TPU v7x, 32 devices: a whole 2x2x4 slice. The times are simulated.
32 devices in a mesh: grp: 2 (over core), gx: 4 (over z), gy: 4 (over y, x).
Axes of the slice: x: 2, y: 2, z: 4, core: 2. Of those that a mesh axis runs over, the one named last changes fastest.
Arguments:
- ocean_state: float32 [4, 60, 64, 512], P(None, None, ('grp', 'gx'), 'gy'), may hold values from -6 to 6
- diffusivity: float32 [64, 512], P(('grp', 'gx'), 'gy'), may hold values from 0.03 to 0.24
- wet_mask: int32 [64, 512], P(('grp', 'gx'), 'gy'), may hold values 0 or 1
- coast_column: int32 [8, 4, 32], P(('grp', 'gx'), 'gy'), may hold values from 0 to 1023, as said below
- coast_slot: int32 [8, 4, 32], P(('grp', 'gx'), 'gy'), may hold values from 0 to 63, as said below
- owner_node: int32 [8, 4, 16, 4], P(('grp', 'gx'), 'gy'), may hold values from -1 to 16383, as said below
- thickness: float32 [1024, 512], P(('grp', 'gx'), 'gy'), may hold values from 1 to 3
- viscosity: float32 [1024, 512], P(('grp', 'gx'), 'gy'), may hold values from 0.5 to 2
- friction: float32 [1024, 512], P(('grp', 'gx'), 'gy'), may hold values from 0.3 to 3
- grounded: int32 [1024, 512], P(('grp', 'gx'), 'gy'), may hold values 0 or 1
- coupling: float32 [1024, 512], P(('grp', 'gx'), 'gy'), may hold values from -1 to 1
- driving: float32 [2, 1024, 512], P(None, ('grp', 'gx'), 'gy'), may hold values from -16 to 16
- first_guess: float32 [2, 1024, 512], P(None, ('grp', 'gx'), 'gy'), may hold values from -2 to 2
Outputs:
- ocean_next: float32 [4, 60, 64, 512], P(None, None, ('grp', 'gx'), 'gy')
- melt_mean: float32 [64, 512], P(('grp', 'gx'), 'gy')
- velocity: float32 [2, 1024, 512], P(None, ('grp', 'gx'), 'gy')
- residual: float32 [2, 1024, 512], P(None, ('grp', 'gx'), 'gy')
Inputs may be any that keep to these rules, and one draw needn't show every extreme that they name: `coast_column`: within a device the 32 numbers are distinct cells of its block. `coast_slot`: within a device the 32 slots are distinct, so at most 4 items go to one peer; every device sends 4 items to some peer. owner_node of an ice device at (peer p, s) is a node of its block exactly when peer p has an item with slot (this device's peer number) * 4 + s, else -1; the nodes of one device are distinct.
All inputs are finite; a program needn't handle non-finite values. No bound on the sum of `wet_mask` or of `grounded` on one device may be relied on, other than what follows from the above.
Results may differ from a plain program's by a relative error of at most 0.00012.
Values sent between devices are 32-bit elements; how exact they have to be, the bound alone decides.
A program may use at most 64 MiB of HBM per device.

v0:
```python
import jax
import jax.numpy as jnp
from jax import lax
from jax.sharding import PartitionSpec as P

NSUB = 4
ITERS = 2


def padded_2(block, sides, width):
    for axis, dim in sides:
        count = lax.axis_size(axis)
        forward = [(i, i + 1) for i in range(count - 1)]
        backward = [(target, source) for source, target in forward]
        low = lax.ppermute(
            lax.slice_in_dim(block, block.shape[dim] - width, None, axis=dim), axis, forward
        )
        high = lax.ppermute(lax.slice_in_dim(block, 0, width, axis=dim), axis, backward)
        block = jnp.concatenate([low, block, high], axis=dim)
    return block


def advance(padded, diff_pad, wet_pad, cover, draft_field):
    fields = padded[:, :, 1:-1, 1:-1]
    row_total = fields.shape[2]
    col_total = fields.shape[3]
    diff_here = diff_pad[1:-1, 1:-1]
    wet_here = wet_pad[1:-1, 1:-1]
    flux_sum = jnp.zeros_like(fields)
    for offset in ((2, 1), (0, 1), (1, 2), (1, 0)):
        diff_side = diff_pad[offset[0] : offset[0] + row_total, offset[1] : offset[1] + col_total]
        wet_side = wet_pad[offset[0] : offset[0] + row_total, offset[1] : offset[1] + col_total]
        side_vals = padded[
            :, :, offset[0] : offset[0] + row_total, offset[1] : offset[1] + col_total
        ]
        weight = 0.5 * (diff_here + diff_side) * wet_here * wet_side
        flux_sum = flux_sum + weight * (side_vals - fields)
    top_temp = fields[0, 0]
    top_salt = fields[1, 0]
    top_east = fields[2, 0]
    top_north = fields[3, 0]
    current_speed = jnp.sqrt(top_east * top_east + top_north * top_north + 0.01)
    freezing = -0.5 * top_salt + 0.3 * draft_field - 0.2
    melt_rate = 0.5 * cover * (top_temp - freezing) * current_speed
    updated = fields + flux_sum
    drag_rate = 0.05 * cover * current_speed
    top_rows = jnp.stack(
        [
            updated[0, 0] - 0.3 * melt_rate,
            updated[1, 0] - 0.2 * melt_rate,
            updated[2, 0] - drag_rate * top_east,
            updated[3, 0] - drag_rate * top_north,
        ]
    )
    updated = updated.at[:, 0].set(top_rows)
    return (updated, melt_rate)


def operator_parts(depth_visc, visc_pad, friction, grounded, coupling):
    weight_east = 0.5 * (depth_visc + visc_pad[2:, 1:-1])
    weight_west = 0.5 * (depth_visc + visc_pad[:-2, 1:-1])
    weight_north = 0.5 * (depth_visc + visc_pad[1:-1, 2:])
    weight_south = 0.5 * (depth_visc + visc_pad[1:-1, :-2])
    base_friction = friction * grounded.astype(jnp.float32) + 0.2
    cross_term = 0.9 * base_friction * coupling
    diagonal = weight_east + weight_west + weight_north + weight_south + base_friction
    return (diagonal, weight_east, weight_west, weight_north, weight_south, cross_term)


def apply_padded(vector_pad, parts):
    diagonal, weight_east, weight_west, weight_north, weight_south, cross_term = parts
    inner = vector_pad[:, 1:-1, 1:-1]
    beside = weight_east * vector_pad[:, 2:, 1:-1] + weight_west * vector_pad[:, :-2, 1:-1]
    beside = (
        beside + weight_north * vector_pad[:, 1:-1, 2:] + weight_south * vector_pad[:, 1:-1, :-2]
    )
    return diagonal * inner - beside + cross_term * inner[::-1]


def ice_rim(stacked):
    return padded_2(stacked, ((("grp", "gx"), 1), ("gy", 2)), 1)


def ice_sum(value):
    return lax.psum(value, ("grp", "gx", "gy"))


def shards(
    ocean_state,
    diffusivity,
    wet_mask,
    coast_column,
    coast_slot,
    owner_node,
    thickness,
    viscosity,
    friction,
    grounded,
    coupling,
    driving,
    first_guess,
):
    field_count, level_count, row_count, col_count = ocean_state.shape
    layers = field_count * level_count
    owner = owner_node[0, 0]
    valid = owner >= 0
    safe_node = jnp.where(valid, owner, 0)
    thick_flat = thickness.reshape(-1)
    draft_send = jnp.where(valid, 0.9 * thick_flat[safe_node], 0.0)
    draft_recv = lax.all_to_all(draft_send, ("gx", "gy"), split_axis=0, concat_axis=0, tiled=True)
    columns = coast_column[0, 0]
    slots = coast_slot[0, 0]
    draft_item = draft_recv.reshape(-1)[slots]
    cell_count = row_count * col_count
    cover = jnp.zeros((cell_count,), jnp.float32).at[columns].set(1.0).reshape(row_count, col_count)
    draft_field = (
        jnp.zeros((cell_count,), jnp.float32)
        .at[columns]
        .set(draft_item)
        .reshape(row_count, col_count)
    )
    wet_field = wet_mask.astype(jnp.float32)
    total = jnp.zeros((row_count, col_count), jnp.float32)
    fields = ocean_state
    stacked = jnp.concatenate(
        [
            fields.reshape(layers, row_count, col_count),
            diffusivity[None],
            wet_field[None],
            cover[None],
            draft_field[None],
        ],
        0,
    )
    padded = padded_2(stacked, ((("grp", "gx"), 1), ("gy", 2)), NSUB)
    current = padded[:layers].reshape(
        field_count, level_count, row_count + 2 * NSUB, col_count + 2 * NSUB
    )
    for substep in range(NSUB):
        stop_row = row_count + 2 * NSUB - substep
        stop_col = col_count + 2 * NSUB - substep
        diff_part = padded[layers, substep:stop_row, substep:stop_col]
        wet_part = padded[layers + 1, substep:stop_row, substep:stop_col]
        cover_part = padded[layers + 2, substep + 1 : stop_row - 1, substep + 1 : stop_col - 1]
        draft_part = padded[layers + 3, substep + 1 : stop_row - 1, substep + 1 : stop_col - 1]
        current, melt_rate = advance(current, diff_part, wet_part, cover_part, draft_part)
        margin = NSUB - substep - 1
        total = total + melt_rate[margin : margin + row_count, margin : margin + col_count]
    fields = current
    melt_mean = total / NSUB
    melt_item = melt_mean.reshape(-1)[columns]
    melt_send = jnp.zeros((owner.size,), jnp.float32).at[slots].set(melt_item).reshape(owner.shape)
    melt_recv = lax.all_to_all(melt_send, ("gx", "gy"), split_axis=0, concat_axis=0, tiled=True)
    melt_node = (
        jnp.zeros((thick_flat.shape[0],), jnp.float32)
        .at[safe_node.reshape(-1)]
        .add(melt_recv.reshape(-1))
    )
    thinned = thickness * jnp.exp(-0.3 * melt_node.reshape(thickness.shape))
    depth_visc = viscosity * thinned
    padded_first = ice_rim(jnp.concatenate([depth_visc[None], first_guess], 0))
    parts = operator_parts(depth_visc, padded_first[0], friction, grounded, coupling)
    rhs = driving * thinned
    velocity = first_guess
    residual = rhs - apply_padded(padded_first[1:], parts)
    precond = residual / parts[0]
    norm_now = ice_sum(jnp.sum(residual * precond))
    direction = precond
    for iteration in range(ITERS):
        image = apply_padded(ice_rim(direction), parts)
        step_size = norm_now / ice_sum(jnp.sum(direction * image))
        velocity = velocity + step_size * direction
        residual = residual - step_size * image
        if iteration + 1 < ITERS:
            precond = residual / parts[0]
            norm_next = ice_sum(jnp.sum(residual * precond))
            direction = precond + norm_next / norm_now * direction
            norm_now = norm_next
    return (fields, melt_mean, velocity, residual)


def solution(mesh):
    in_specs = (
        P(None, None, ("grp", "gx"), "gy"),
        P(("grp", "gx"), "gy"),
        P(("grp", "gx"), "gy"),
        P(("grp", "gx"), "gy", None),
        P(("grp", "gx"), "gy", None),
        P(("grp", "gx"), "gy", None, None),
        P(("grp", "gx"), "gy"),
        P(("grp", "gx"), "gy"),
        P(("grp", "gx"), "gy"),
        P(("grp", "gx"), "gy"),
        P(("grp", "gx"), "gy"),
        P(None, ("grp", "gx"), "gy"),
        P(None, ("grp", "gx"), "gy"),
    )
    out_specs = (
        P(None, None, ("grp", "gx"), "gy"),
        P(("grp", "gx"), "gy"),
        P(None, ("grp", "gx"), "gy"),
        P(None, ("grp", "gx"), "gy"),
    )
    return jax.shard_map(shards, mesh=mesh, in_specs=in_specs, out_specs=out_specs, check_vma=False)
```

profile of v0, /device:TPU:0, one launch (start us, length us, event | category | flops | bytes accessed | tf_op | source)
XLA Modules:
  0.0 292.9 jit_solution(1306084586480091824)
XLA Ops:
  0.6 0.7 fusion.168
  1.3 0.7 compare_select_fusion
  2.2 1.7 gather_fusion
  4.1 0.7 copy.60
  4.8 8.3 %all-to-all-start = ((f32[16,1,4]{2,1,0:T(1,128)}), f32[16,1,4]{2,1,0:T(1,128)S(1)}, u32[]{:S(2)}, u32[]{:S(2)}) async-start(f32[16,1,4]{2,1,0:T(1,128)} %copy.60), calls=%async_computation | async-start | bytes 16384 | tf_op jit(solution)/shard_map/all_to_all | solution.py:110
  13.2 0.7 scatter_custom_fusion
  14.0 6.3 %all-to-all-done = f32[16,1,4]{2,1,0:T(1,128)S(1)} async-done(((f32[16,1,4]{2,1,0:T(1,128)}), f32[16,1,4]{2,1,0:T(1,128)S(1)}, u32[]{:S(2)}, u32[]{:S(2)}) %all-to-all-start) | async-done | bytes 288 | tf_op jit(solution)/shard_map/all_to_all | solution.py:110
  21.6 0.7 gather_fusion.1
  22.3 0.7 scatter_custom_fusion.1
  23.2 2.5 collective-permute-start
  25.7 1.3 collective-permute-start.1
  27.0 10.5 %collective-permute-done = f32[244,4,128]{2,1,0:T(4,128)S(1)} collective-permute-done((f32[244,4,128]{2,1,0:T(4,128)S(1)}, f32[244,4,128]{2,1,0:T(4,128)S(1)}, u32[]{:S(2)}, u32[]{:S(2)}) %collective-permute-start) | collective-permute-done | bytes 499744 | tf_op jit(solution)/shard_map/ppermute | solution.py:15
  37.5 6.8 %collective-permute-done.1 = f32[244,4,128]{2,1,0:T(4,128)S(1)} collective-permute-done((f32[244,4,128]{2,1,0:T(4,128)S(1)}, f32[244,4,128]{2,1,0:T(4,128)S(1)}, u32[]{:S(2)}, u32[]{:S(2)}) %collective-permute-start.1) | collective-permute-done | bytes 499744 | tf_op jit(solution)/shard_map/ppermute | solution.py:18
  44.4 0.8 copy-done.4
  45.5 1.9 fusion.185
  47.5 3.1 %copy.61 = f32[244,16,4]{0,1,2:T(8,128)} copy(f32[244,16,4]{2,1,0:T(8,128)} %get-tuple-element.114) | data formatting | bytes 124928 | tf_op jit(solution)/shard_map/slice | solution.py:16
  50.6 3.1 %collective-permute-start.2 = (f32[244,16,4]{0,1,2:T(8,128)}, f32[244,16,4]{0,1,2:T(8,128)}, u32[]{:S(2)}, u32[]{:S(2)}) collective-permute-start(f32[244,16,4]{0,1,2:T(8,128)} %copy.61), channel_id=1, source_target_pairs={{0,1},{1,2},{2,3},{4,5},{5,6},{6,7},{8,9},{9,10},{10,11},{12,13},{... | collective-permute-start | bytes 187400 | tf_op jit(solution)/shard_map/ppermute | solution.py:15
  53.6 1.6 copy.62
  55.3 1.3 collective-permute-start.3
  56.7 2.0 copy.63
  58.8 3.0 %collective-permute-done.3 = f32[244,16,4]{0,1,2:T(8,128)} collective-permute-done((f32[244,16,4]{0,1,2:T(8,128)}, f32[244,16,4]{0,1,2:T(8,128)}, u32[]{:S(2)}, u32[]{:S(2)}) %collective-permute-start.3) | collective-permute-done | bytes 62496 | tf_op jit(solution)/shard_map/ppermute | solution.py:18
  61.7 3.2 %copy.64 = f32[244,16,4]{2,1,0:T(8,128)} copy(f32[244,16,4]{0,1,2:T(8,128)} %collective-permute-done.3) | data formatting | bytes 124928 | tf_op jit(solution)/shard_map/ppermute | solution.py:18
  64.9 4.4 %pad_maximum_fusion = f32[244,16,136]{2,1,0:T(8,128)S(1)} fusion(f32[244,16,4]{2,1,0:T(8,128)} %copy.64, f32[244,4,128]{2,1,0:T(4,128)} %copy-done.4, f32[244,8,128]{2,1,0:T(8,128)S(1)} %constant_dynamic-update-slice_fusion, f32[244,4,128]{2,1,0:T(4,128)S(1)} %collective-permute-done, f32[244,16,4]{2,1,0:T(8,128)S(1)} %copy.63), kind=kLoop, calls=%fused_computation.7 | loop fusion | flops 2123776 | bytes 4247552 | tf_op jit(solution)/shard_map/concatenate | solution.py:19
  69.9 1.0 copy-done.1
  71.2 4.4 %fusion.18 = f32[4,60,14,134]{3,2,1,0:T(8,128)S(1)} fusion(f32[4,60,16,136]{3,2,1,0:T(8,128)S(1)} %bitcast.398, f32[14,134]{1,0:T(8,128)S(1)} %get-tuple-element.157, f32[14,134]{1,0:T(8,128)S(1)} %get-tuple-element.155, f32[14,134]{1,0:T(8,128)S(1)} %get-tuple-element.156, f32[14,134]{1,0:T(8,128)S(1)} %get-tuple-element.154), kind=kLoop, calls=%fused_computation.35 | loop fusion | flops 5402880 | bytes 10835776 | tf_op jit(solution)/shard_map/add | solution.py:45
  76.2 4.3 %fusion.10 = f32[4,60,12,132]{3,2,1,0:T(8,128)S(1)} fusion(f32[4,60,14,134]{3,2,1,0:T(8,128)S(1)} %constant_dynamic-update-slice_fusion.7, f32[12,132]{1,0:T(8,128)S(1)} %get-tuple-element.153, f32[12,132]{1,0:T(8,128)S(1)} %get-tuple-element.151, f32[12,132]{1,0:T(8,128)S(1)} %get-tuple-element.152, f32[12,132]{1,0:T(8,128)S(1)} %get-tuple-element.150), kind=kLoop, calls=%fused_computation.23 | loop fusion | flops 4561920 | bytes 9149184 | tf_op jit(solution)/shard_map/add | solution.py:45
  80.9 4.3 %fusion.2 = f32[4,60,10,130]{3,2,1,0:T(8,128)S(1)} fusion(f32[4,60,12,132]{3,2,1,0:T(8,128)S(1)} %constant_dynamic-update-slice_fusion.6, f32[10,130]{1,0:T(8,128)S(1)} %get-tuple-element.149, f32[10,130]{1,0:T(8,128)S(1)} %get-tuple-element.147, f32[10,130]{1,0:T(8,128)S(1)} %get-tuple-element.148, f32[10,130]{1,0:T(8,128)S(1)} %get-tuple-element.146), kind=kLoop, calls=%fused_computation.11 | loop fusion | flops 3744000 | bytes 7508800 | tf_op jit(solution)/shard_map/add | solution.py:45
  85.4 1.1 fusion.74
  87.2 0.7 gather_fusion.2
  87.9 0.7 scatter_custom_fusion.2
  88.6 0.7 all_to_all.11
  89.3 3.5 %all-to-all-start.1 = ((f32[16,1,4]{2,1,0:T(1,128)}), f32[16,1,4]{2,1,0:T(1,128)S(1)}, u32[]{:S(2)}, u32[]{:S(2)}) async-start(f32[16,1,4]{2,1,0:T(1,128)} %bitcast.84), calls=%async_computation.1 | async-start | bytes 16384 | tf_op jit(solution)/shard_map/all_to_all | solution.py:153
  92.8 7.2 %all-to-all-done.1 = f32[16,1,4]{2,1,0:T(1,128)S(1)} async-done(((f32[16,1,4]{2,1,0:T(1,128)}), f32[16,1,4]{2,1,0:T(1,128)S(1)}, u32[]{:S(2)}, u32[]{:S(2)}) %all-to-all-start.1) | async-done | bytes 288 | tf_op jit(solution)/shard_map/all_to_all | solution.py:153
  100.7 0.9 scatter_custom_fusion.3
  101.6 0.9 fusion.180
  102.5 2.5 collective-permute-start.4
  105.0 1.3 collective-permute-start.5
  106.4 4.1 %collective-permute-done.5 = f32[3,1,128]{2,1,0:T(1,128)S(1)} collective-permute-done((f32[3,1,128]{2,1,0:T(1,128)S(1)}, f32[3,1,128]{2,1,0:T(1,128)S(1)}, u32[]{:S(2)}, u32[]{:S(2)}) %collective-permute-start.5) | collective-permute-done | bytes 1568 | tf_op jit(solution)/shard_map/ppermute | solution.py:18
  110.6 2.5 collective-permute-start.6
  113.1 1.3 collective-permute-start.7
  115.0 1.4 collective-permute-done.6
  116.4 4.9 %collective-permute-done.7 = f32[3,130,1]{2,1,0:T(8,128)S(1)} collective-permute-done((f32[3,130,1]{2,1,0:T(8,128)S(1)}, f32[3,130,1]{2,1,0:T(8,128)S(1)}, u32[]{:S(2)}, u32[]{:S(2)}) %collective-permute-start.7) | collective-permute-done | bytes 1592 | tf_op jit(solution)/shard_map/ppermute | solution.py:18
  121.5 1.0 add_add_fusion
  122.7 2.0 collective-permute-start.9
  124.7 1.3 collective-permute-start.8
  126.0 6.9 %fusion.26 = f32[4,60,8,128]{3,2,1,0:T(8,128)S(1)} fusion(f32[4,60,10,130]{3,2,1,0:T(8,128)} %constant_dynamic-update-slice_fusion.5, f32[8,128]{1,0:T(8,128)S(1)} %get-tuple-element.145, f32[8,128]{1,0:T(8,128)S(1)} %get-tuple-element.143, f32[8,128]{1,0:T(8,128)S(1)} %get-tuple-element.144, f32[8,128]{1,0:T(8,128)S(1)} %get-tuple-element.142), kind=kLoop, calls=%fused_computation.48 | loop fusion | flops 2949120 | bytes 5914624 | tf_op jit(solution)/shard_map/add | solution.py:45
  133.0 1.3 collective-permute-start.10
  134.3 4.9 %collective-permute-start.11 = (f32[2,130,1]{2,1,0:T(8,128)S(1)}, f32[2,130,1]{2,1,0:T(8,128)S(1)}, u32[]{:S(2)}, u32[]{:S(2)}) collective-permute-start(f32[2,130,1]{2,1,0:T(8,128)S(1)} %get-tuple-element.127), channel_id=1, source_target_pairs={{0,1},{1,2},{2,3},{4,5},{5,6},{6,7},{8,9},{9,10},{10,11},{12,13},{... | collective-permute-start | bytes 3128 | tf_op jit(solution)/shard_map/ppermute | solution.py:15
  139.3 1.3 collective-permute-done.10
  140.7 1.8 collective-permute-done.11
  142.5 0.8 multiply_reduce_fusion.2
  143.3 42.8 %all-reduce = (f32[]{:T(128)}, f32[]{:T(128)}) all-reduce(f32[]{:T(128)} %get-tuple-element.57, f32[]{:T(128)} %get-tuple-element.56), channel_id=1, replica_groups=mesh['grp'=2,'gx'=4,'gy'=4] {'grp','gx','gy'}, use_global_device_ids=true, to_apply=%region_5.6 | all-reduce | flops 2 | bytes 16 | tf_op jit(solution)/shard_map/psum | solution.py:85
  188.0 40.8 %psum.30 = f32[]{:T(128)} all-reduce(f32[]{:T(128)} %get-tuple-element.62), channel_id=1, replica_groups=mesh['grp'=2,'gx'=4,'gy'=4] {'grp','gx','gy'}, use_global_device_ids=true, to_apply=%region_9.10 | all-reduce | flops 1 | bytes 8 | tf_op jit(solution)/shard_map/psum | solution.py:85
  230.2 3.5 %collective-permute-start.13 = (f32[2,1,128]{2,1,0:T(1,128)S(1)}, f32[2,1,128]{2,1,0:T(1,128)S(1)}, u32[]{:S(2)}, u32[]{:S(2)}) collective-permute-start(f32[2,1,128]{2,1,0:T(1,128)S(1)} %get-tuple-element.128), channel_id=1, source_target_pairs={{0,4},{4,8},{8,12},{12,16},{16,20},{20,24},{24,28},{1,5},{5,9},{9,... | collective-permute-start | bytes 3080 | tf_op jit(solution)/shard_map/ppermute | solution.py:15
  233.7 1.3 collective-permute-start.12
  235.0 4.1 %collective-permute-done.12 = f32[2,1,128]{2,1,0:T(1,128)S(1)} collective-permute-done((f32[2,1,128]{2,1,0:T(1,128)S(1)}, f32[2,1,128]{2,1,0:T(1,128)S(1)}, u32[]{:S(2)}, u32[]{:S(2)}) %collective-permute-start.12) | collective-permute-done | bytes 1056 | tf_op jit(solution)/shard_map/ppermute | solution.py:18
  239.3 1.3 collective-permute-start.14
  240.6 4.8 %collective-permute-start.15 = (f32[2,130,1]{2,1,0:T(8,128)S(1)}, f32[2,130,1]{2,1,0:T(8,128)S(1)}, u32[]{:S(2)}, u32[]{:S(2)}) collective-permute-start(f32[2,130,1]{2,1,0:T(8,128)S(1)} %get-tuple-element.125), channel_id=1, source_target_pairs={{0,1},{1,2},{2,3},{4,5},{5,6},{6,7},{8,9},{9,10},{10,11},{12,13},{... | collective-permute-start | bytes 3128 | tf_op jit(solution)/shard_map/ppermute | solution.py:15
  245.4 1.1 collective-permute-done.14
  246.5 1.5 collective-permute-done.15
  248.0 0.8 multiply_reduce_fusion
  248.8 41.4 %psum.31 = f32[]{:T(128)} all-reduce(f32[]{:T(128)} %get-tuple-element.60), channel_id=1, replica_groups=mesh['grp'=2,'gx'=4,'gy'=4] {'grp','gx','gy'}, use_global_device_ids=true, to_apply=%region_11.12 | all-reduce | flops 1 | bytes 8 | tf_op jit(solution)/shard_map/psum | solution.py:85
  291.5 0.7 multiply_add_fusion
  292.2 0.7 multiply_subtract_fusion
  (101 shorter events, 7.9 us)
Async XLA Ops:
  2.2 1.9 copy-start.12
  2.2 10.9 %copy-start.15 = (s32[1,1,32]{2,1,0:T(1,128)S(1)}, s32[1,1,32]{2,1,0:T(1,128)}, u32[]{:S(2)}) copy-start(s32[1,1,32]{2,1,0:T(1,128)} %param.25) | copy-start | bytes 388
  2.2 11.0 %copy-start.9 = (f32[4,60,8,128]{3,2,1,0:T(8,128)S(1)}, f32[4,60,8,128]{3,2,1,0:T(8,128)}, u32[]{:S(2)}) copy-start(f32[4,60,8,128]{3,2,1,0:T(8,128)} %param.21) | copy-start | bytes 2949124
  2.2 11.7 %copy-start.13 = (f32[8,128]{1,0:T(8,128)S(1)}, f32[8,128]{1,0:T(8,128)}, u32[]{:S(2)}) copy-start(f32[8,128]{1,0:T(8,128)} %param.22) | copy-start | bytes 12292
  2.2 11.7 %copy-start.14 = (s32[8,128]{1,0:T(8,128)S(1)}, s32[8,128]{1,0:T(8,128)}, u32[]{:S(2)}) copy-start(s32[8,128]{1,0:T(8,128)} %param.23) | copy-start | bytes 12292
  4.8 15.5 %all-to-all-start = ((f32[16,1,4]{2,1,0:T(1,128)}), f32[16,1,4]{2,1,0:T(1,128)S(1)}, u32[]{:S(2)}, u32[]{:S(2)}) async-start(f32[16,1,4]{2,1,0:T(1,128)} %copy.60), calls=%async_computation | async-start | bytes 16384 | tf_op jit(solution)/shard_map/all_to_all | solution.py:110
  23.2 14.3 %collective-permute-start = (f32[244,4,128]{2,1,0:T(4,128)S(1)}, f32[244,4,128]{2,1,0:T(4,128)S(1)}, u32[]{:S(2)}, u32[]{:S(2)}) collective-permute-start(f32[244,4,128]{2,1,0:T(4,128)S(1)} %get-tuple-element.118), channel_id=1, source_target_pairs={{0,4},{4,8},{8,12},{12,16},{16,20},{20,24},{24,28},{1,5},{5,9},{9,... | collective-permute-start | bytes 1499144 | tf_op jit(solution)/shard_map/ppermute | solution.py:15
  25.7 18.6 %collective-permute-start.1 = (f32[244,4,128]{2,1,0:T(4,128)S(1)}, f32[244,4,128]{2,1,0:T(4,128)S(1)}, u32[]{:S(2)}, u32[]{:S(2)}) collective-permute-start(f32[244,4,128]{2,1,0:T(4,128)S(1)} %get-tuple-element.119), channel_id=1, source_target_pairs={{4,0},{8,4},{12,8},{16,12},{20,16},{24,20},{28,24},{5,1},{9,5},{13... | collective-permute-start | bytes 1499144 | tf_op jit(solution)/shard_map/ppermute | solution.py:18
  37.5 47.7 %copy-start.3 = (f32[244,4,128]{2,1,0:T(4,128)}, f32[244,4,128]{2,1,0:T(4,128)S(1)}, u32[]{:S(2)}) copy-start(f32[244,4,128]{2,1,0:T(4,128)S(1)} %collective-permute-done) | copy-start | bytes 1499140
  44.4 0.8 copy-start.4
  50.6 6.2 %collective-permute-start.2 = (f32[244,16,4]{0,1,2:T(8,128)}, f32[244,16,4]{0,1,2:T(8,128)}, u32[]{:S(2)}, u32[]{:S(2)}) collective-permute-start(f32[244,16,4]{0,1,2:T(8,128)} %copy.61), channel_id=1, source_target_pairs={{0,1},{1,2},{2,3},{4,5},{5,6},{6,7},{8,9},{9,10},{10,11},{12,13},{... | collective-permute-start | bytes 187400 | tf_op jit(solution)/shard_map/ppermute | solution.py:15
  55.3 6.5 %collective-permute-start.3 = (f32[244,16,4]{0,1,2:T(8,128)}, f32[244,16,4]{0,1,2:T(8,128)}, u32[]{:S(2)}, u32[]{:S(2)}) collective-permute-start(f32[244,16,4]{0,1,2:T(8,128)} %copy.62), channel_id=1, source_target_pairs={{1,0},{2,1},{3,2},{5,4},{6,5},{7,6},{9,8},{10,9},{11,10},{13,12},{... | collective-permute-start | bytes 187400 | tf_op jit(solution)/shard_map/ppermute | solution.py:18
  69.3 1.6 copy-start.1
  69.4 1.6 copy-start.5
  85.2 1.9 copy-start.6
  85.3 16.3 %copy-start = (f32[128,128]{1,0:T(8,128)S(1)}, f32[128,128]{1,0:T(8,128)}, u32[]{:S(2)}) copy-start(f32[128,128]{1,0:T(8,128)} %param.27) | copy-start | bytes 196612
  85.3 17.2 %copy-start.7 = (f32[2,128,128]{2,1,0:T(8,128)S(1)}, f32[2,128,128]{2,1,0:T(8,128)}, u32[]{:S(2)}) copy-start(f32[2,128,128]{2,1,0:T(8,128)} %param.33) | copy-start | bytes 393220
  85.4 36.1 %copy-start.11 = (f32[128,128]{1,0:T(8,128)S(1)}, f32[128,128]{1,0:T(8,128)}, u32[]{:S(2)}) copy-start(f32[128,128]{1,0:T(8,128)} %param.29) | copy-start | bytes 196612
  85.4 37.1 %copy-start.10 = (f32[2,128,128]{2,1,0:T(8,128)S(1)}, f32[2,128,128]{2,1,0:T(8,128)}, u32[]{:S(2)}) copy-start(f32[2,128,128]{2,1,0:T(8,128)} %param.32) | copy-start | bytes 393220
  87.2 45.7 %copy-start.2 = (f32[8,128]{1,0:T(8,128)}, f32[8,128]{1,0:T(8,128)S(1)}, u32[]{:S(2)}) copy-start(f32[8,128]{1,0:T(8,128)S(1)} %fusion.134) | copy-start | bytes 12292
  89.3 10.6 %all-to-all-start.1 = ((f32[16,1,4]{2,1,0:T(1,128)}), f32[16,1,4]{2,1,0:T(1,128)S(1)}, u32[]{:S(2)}, u32[]{:S(2)}) async-start(f32[16,1,4]{2,1,0:T(1,128)} %bitcast.84), calls=%async_computation.1 | async-start | bytes 16384 | tf_op jit(solution)/shard_map/all_to_all | solution.py:153
  102.5 3.9 %collective-permute-start.4 = (f32[3,1,128]{2,1,0:T(1,128)S(1)}, f32[3,1,128]{2,1,0:T(1,128)S(1)}, u32[]{:S(2)}, u32[]{:S(2)}) collective-permute-start(f32[3,1,128]{2,1,0:T(1,128)S(1)} %get-tuple-element.122), channel_id=1, source_target_pairs={{0,4},{4,8},{8,12},{12,16},{16,20},{20,24},{24,28},{1,5},{5,9},{9,... | collective-permute-start | bytes 4616 | tf_op jit(solution)/shard_map/ppermute | solution.py:15
  105.0 5.5 %collective-permute-start.5 = (f32[3,1,128]{2,1,0:T(1,128)S(1)}, f32[3,1,128]{2,1,0:T(1,128)S(1)}, u32[]{:S(2)}, u32[]{:S(2)}) collective-permute-start(f32[3,1,128]{2,1,0:T(1,128)S(1)} %get-tuple-element.123), channel_id=1, source_target_pairs={{4,0},{8,4},{12,8},{16,12},{20,16},{24,20},{28,24},{5,1},{9,5},{13... | collective-permute-start | bytes 4616 | tf_op jit(solution)/shard_map/ppermute | solution.py:18
  110.6 5.8 %collective-permute-start.6 = (f32[3,130,1]{2,1,0:T(8,128)S(1)}, f32[3,130,1]{2,1,0:T(8,128)S(1)}, u32[]{:S(2)}, u32[]{:S(2)}) collective-permute-start(f32[3,130,1]{2,1,0:T(8,128)S(1)} %get-tuple-element.120), channel_id=1, source_target_pairs={{0,1},{1,2},{2,3},{4,5},{5,6},{6,7},{8,9},{9,10},{10,11},{12,13},{... | collective-permute-start | bytes 4688 | tf_op jit(solution)/shard_map/ppermute | solution.py:15
  113.1 8.2 %collective-permute-start.7 = (f32[3,130,1]{2,1,0:T(8,128)S(1)}, f32[3,130,1]{2,1,0:T(8,128)S(1)}, u32[]{:S(2)}, u32[]{:S(2)}) collective-permute-start(f32[3,130,1]{2,1,0:T(8,128)S(1)} %get-tuple-element.121), channel_id=1, source_target_pairs={{1,0},{2,1},{3,2},{5,4},{6,5},{7,6},{9,8},{10,9},{11,10},{13,12},{... | collective-permute-start | bytes 4688 | tf_op jit(solution)/shard_map/ppermute | solution.py:18
  122.7 10.2 %collective-permute-start.9 = (f32[2,1,128]{2,1,0:T(1,128)S(1)}, f32[2,1,128]{2,1,0:T(1,128)S(1)}, u32[]{:S(2)}, u32[]{:S(2)}) collective-permute-start(f32[2,1,128]{2,1,0:T(1,128)S(1)} %get-tuple-element.130), channel_id=1, source_target_pairs={{0,4},{4,8},{8,12},{12,16},{16,20},{20,24},{24,28},{1,5},{5,9},{9,... | collective-permute-start | bytes 3080 | tf_op jit(solution)/shard_map/ppermute | solution.py:15
  124.7 8.2 %collective-permute-start.8 = (f32[2,1,128]{2,1,0:T(1,128)S(1)}, f32[2,1,128]{2,1,0:T(1,128)S(1)}, u32[]{:S(2)}, u32[]{:S(2)}) collective-permute-start(f32[2,1,128]{2,1,0:T(1,128)S(1)} %get-tuple-element.131), channel_id=1, source_target_pairs={{4,0},{8,4},{12,8},{16,12},{20,16},{24,20},{28,24},{5,1},{9,5},{13... | collective-permute-start | bytes 3080 | tf_op jit(solution)/shard_map/ppermute | solution.py:18
  133.0 7.6 %collective-permute-start.10 = (f32[2,130,1]{2,1,0:T(8,128)S(1)}, f32[2,130,1]{2,1,0:T(8,128)S(1)}, u32[]{:S(2)}, u32[]{:S(2)}) collective-permute-start(f32[2,130,1]{2,1,0:T(8,128)S(1)} %get-tuple-element.126), channel_id=1, source_target_pairs={{1,0},{2,1},{3,2},{5,4},{6,5},{7,6},{9,8},{10,9},{11,10},{13,12},{... | collective-permute-start | bytes 3128 | tf_op jit(solution)/shard_map/ppermute | solution.py:18
  134.3 8.1 %collective-permute-start.11 = (f32[2,130,1]{2,1,0:T(8,128)S(1)}, f32[2,130,1]{2,1,0:T(8,128)S(1)}, u32[]{:S(2)}, u32[]{:S(2)}) collective-permute-start(f32[2,130,1]{2,1,0:T(8,128)S(1)} %get-tuple-element.127), channel_id=1, source_target_pairs={{0,1},{1,2},{2,3},{4,5},{5,6},{6,7},{8,9},{9,10},{10,11},{12,13},{... | collective-permute-start | bytes 3128 | tf_op jit(solution)/shard_map/ppermute | solution.py:15
  230.2 4.8 %collective-permute-start.13 = (f32[2,1,128]{2,1,0:T(1,128)S(1)}, f32[2,1,128]{2,1,0:T(1,128)S(1)}, u32[]{:S(2)}, u32[]{:S(2)}) collective-permute-start(f32[2,1,128]{2,1,0:T(1,128)S(1)} %get-tuple-element.128), channel_id=1, source_target_pairs={{0,4},{4,8},{8,12},{12,16},{16,20},{20,24},{24,28},{1,5},{5,9},{9,... | collective-permute-start | bytes 3080 | tf_op jit(solution)/shard_map/ppermute | solution.py:15
  233.7 5.5 %collective-permute-start.12 = (f32[2,1,128]{2,1,0:T(1,128)S(1)}, f32[2,1,128]{2,1,0:T(1,128)S(1)}, u32[]{:S(2)}, u32[]{:S(2)}) collective-permute-start(f32[2,1,128]{2,1,0:T(1,128)S(1)} %get-tuple-element.129), channel_id=1, source_target_pairs={{4,0},{8,4},{12,8},{16,12},{20,16},{24,20},{28,24},{5,1},{9,5},{13... | collective-permute-start | bytes 3080 | tf_op jit(solution)/shard_map/ppermute | solution.py:18
  239.3 7.2 %collective-permute-start.14 = (f32[2,130,1]{2,1,0:T(8,128)S(1)}, f32[2,130,1]{2,1,0:T(8,128)S(1)}, u32[]{:S(2)}, u32[]{:S(2)}) collective-permute-start(f32[2,130,1]{2,1,0:T(8,128)S(1)} %get-tuple-element.124), channel_id=1, source_target_pairs={{1,0},{2,1},{3,2},{5,4},{6,5},{7,6},{9,8},{10,9},{11,10},{13,12},{... | collective-permute-start | bytes 3128 | tf_op jit(solution)/shard_map/ppermute | solution.py:18
  240.6 7.4 %collective-permute-start.15 = (f32[2,130,1]{2,1,0:T(8,128)S(1)}, f32[2,130,1]{2,1,0:T(8,128)S(1)}, u32[]{:S(2)}, u32[]{:S(2)}) collective-permute-start(f32[2,130,1]{2,1,0:T(8,128)S(1)} %get-tuple-element.125), channel_id=1, source_target_pairs={{0,1},{1,2},{2,3},{4,5},{5,6},{6,7},{8,9},{9,10},{10,11},{12,13},{... | collective-permute-start | bytes 3128 | tf_op jit(solution)/shard_map/ppermute | solution.py:15
  245.4 47.5 %copy-start.8 = (f32[4,60,8,128]{3,2,1,0:T(8,128)}, f32[4,60,8,128]{3,2,1,0:T(8,128)S(1)}, u32[]{:S(2)}) copy-start(f32[4,60,8,128]{3,2,1,0:T(8,128)S(1)} %fusion.107) | copy-start | bytes 2949124
where the time goes:
time: 294 us; the launch traced here: 293 us
  blocking collectives  125 us (43%)
  waiting for transfers between devices  54 us (18%)
  starting transfers between devices  47.8 us (16%)
  other arithmetic  37.5 us (13%)
  local copies, waits for them, and re-layouts  23.2 us (8%)
  between operations  5.47 us (2%)
    psum x3, blocking collectives, ice_sum(): return lax.psum(value, ('grp', 'gx', 'gy'))  125 us
    ppermute x8, starting transfers between devices, padded_2(): lax.ppermute(lax.slice_in_dim(block, block.shape[dim] - width, None, axis...  25.7 us
    ppermute x8, waiting for transfers between devices, padded_2(): lax.ppermute(lax.slice_in_dim(block, 0, width, axis=dim), axis, backward)  25.4 us
    add x4, other arithmetic, advance(): updated = fields + flux_sum  19.9 us
    ppermute x8, waiting for transfers between devices, padded_2(): lax.ppermute(lax.slice_in_dim(block, block.shape[dim] - width, None, axis...  15.1 us
    ppermute x8, starting transfers between devices, padded_2(): lax.ppermute(lax.slice_in_dim(block, 0, width, axis=dim), axis, backward)  10.3 us
    all_to_all x1, starting transfers between devices, shards(): lax.all_to_all(draft_send, ('gx', 'gy'), split_axis=0, concat_axis=0, til...  8.31 us
    all_to_all x1, waiting for transfers between devices, shards(): lax.all_to_all(melt_send, ('gx', 'gy'), split_axis=0, concat_axis=0, tile...  7.15 us
  transfers between devices with their start and end apart: 18, of which 13 were waited for; matrix products, arithmetic and copies ran while one was open for 4% of the time, Pallas kernels for 0%

commit v1 on v0

--- a/solution.py
+++ b/solution.py
@@ -1,10 +1,13 @@
 import jax
 import jax.numpy as jnp
 from jax import lax
+from jax.experimental import pallas as pl
+from jax.experimental.pallas import tpu as pltpu
 from jax.sharding import PartitionSpec as P
 
 NSUB = 4
-ITERS = 2
+CAP = 4
+MESH = pl.DeviceIdType.MESH
 
 
 def padded_2(block, sides, width):
@@ -56,33 +59,350 @@
     return (updated, melt_rate)
 
 
-def operator_parts(depth_visc, visc_pad, friction, grounded, coupling):
-    weight_east = 0.5 * (depth_visc + visc_pad[2:, 1:-1])
-    weight_west = 0.5 * (depth_visc + visc_pad[:-2, 1:-1])
-    weight_north = 0.5 * (depth_visc + visc_pad[1:-1, 2:])
-    weight_south = 0.5 * (depth_visc + visc_pad[1:-1, :-2])
-    base_friction = friction * grounded.astype(jnp.float32) + 0.2
-    cross_term = 0.9 * base_friction * coupling
-    diagonal = weight_east + weight_west + weight_north + weight_south + base_friction
-    return (diagonal, weight_east, weight_west, weight_north, weight_south, cross_term)
-
-
-def apply_padded(vector_pad, parts):
-    diagonal, weight_east, weight_west, weight_north, weight_south, cross_term = parts
-    inner = vector_pad[:, 1:-1, 1:-1]
-    beside = weight_east * vector_pad[:, 2:, 1:-1] + weight_west * vector_pad[:, :-2, 1:-1]
-    beside = (
-        beside + weight_north * vector_pad[:, 1:-1, 2:] + weight_south * vector_pad[:, 1:-1, :-2]
-    )
-    return diagonal * inner - beside + cross_term * inner[::-1]
-
-
-def ice_rim(stacked):
-    return padded_2(stacked, ((("grp", "gx"), 1), ("gy", 2)), 1)
-
-
-def ice_sum(value):
-    return lax.psum(value, ("grp", "gx", "gy"))
+def device_tools(names):
+    sizes = {name: lax.axis_size(name) for name in names}
+    n_grp, n_gx, n_gy = sizes["grp"], sizes["gx"], sizes["gy"]
+    grp, gx, gy = lax.axis_index("grp"), lax.axis_index("gx"), lax.axis_index("gy")
+    bx = grp * n_gx + gx
+
+    def at_row(row):
+        return (row // n_gx, row % n_gx, gy)
+
+    sides = (
+        (bx > 0, at_row(jnp.maximum(bx - 1, 0))),
+        (bx < n_grp * n_gx - 1, at_row(jnp.minimum(bx + 1, n_grp * n_gx - 1))),
+        (gy > 0, (grp, gx, jnp.maximum(gy - 1, 0))),
+        (gy < n_gy - 1, (grp, gx, jnp.minimum(gy + 1, n_gy - 1))),
+    )
+    return grp, gx, gy, n_grp, n_gx, n_gy, sides
+
+
+def signal(semaphore, target):
+    pl.semaphore_signal(semaphore, inc=1, device_id=target, device_id_type=MESH)
+
+
+def enter(tools):
+    grp, gx, gy, n_grp, n_gx, n_gy, sides = tools
+    peers = n_gx * n_gy
+    me = gx * n_gy + gy
+    barrier = pltpu.get_barrier_semaphore()
+
+    def greet(i, carry):
+        peer = lax.rem(me + i, peers)
+        signal(barrier, (grp, peer // n_gy, peer % n_gy))
+        return carry
+
+    lax.fori_loop(1, peers, greet, 0)
+    for i in range(1, n_grp):
+        signal(barrier, (lax.rem(grp + i, n_grp), gx, gy))
+    cross_low = jnp.logical_and(gx == 0, grp > 0)
+    cross_high = jnp.logical_and(gx == n_gx - 1, grp < n_grp - 1)
+
+    @pl.when(cross_low)
+    def _():
+        signal(barrier, sides[0][1])
+
+    @pl.when(cross_high)
+    def _():
+        signal(barrier, sides[1][1])
+
+    extra = cross_low.astype(jnp.int32) + cross_high.astype(jnp.int32)
+    pl.semaphore_wait(barrier, peers - 1 + n_grp - 1 + extra)
+
+
+class Gather:
+    def __init__(self, tools, source, rows, send_sems, recv_sems):
+        self.tools, self.source, self.rows = tools, source, rows
+        self.send_sems, self.recv_sems = send_sems, recv_sems
+        self.peers = tools[4] * tools[5]
+        self.me = tools[1] * tools[5] + tools[2]
+
+    def copy(self, peer, slot):
+        n_gy = self.tools[5]
+        return pltpu.make_async_remote_copy(
+            src_ref=self.source,
+            dst_ref=self.rows.at[slot],
+            send_sem=self.send_sems.at[peer],
+            recv_sem=self.recv_sems.at[slot],
+            device_id=(self.tools[0], peer // n_gy, peer % n_gy),
+            device_id_type=MESH,
+        )
+
+    def start(self, block):
+        self.source[...] = block
+        self.rows[self.me] = block
+
+        def step(i, carry):
+            self.copy(lax.rem(self.me + i, self.peers), self.me).start()
+            return carry
+
+        lax.fori_loop(1, self.peers, step, 0)
+
+    def wait(self):
+        def step(i, carry):
+            peer = lax.rem(self.me + i, self.peers)
+            self.copy(peer, peer).wait_recv()
+            return carry
+
+        lax.fori_loop(1, self.peers, step, 0)
+
+    def finish(self):
+        def step(i, carry):
+            peer = lax.rem(self.me + i, self.peers)
+            self.copy(peer, peer).wait_send()
+            return carry
+
+        lax.fori_loop(1, self.peers, step, 0)
+
+
+class Rim:
+    def __init__(self, tools, source, landing, send_sems, recv_sems):
+        self.sides = tools[6]
+        self.source, self.landing = source, landing
+        self.send_sems, self.recv_sems = send_sems, recv_sems
+
+    def copy(self, side, slot):
+        return pltpu.make_async_remote_copy(
+            src_ref=self.source.at[side],
+            dst_ref=self.landing.at[slot],
+            send_sem=self.send_sems.at[side],
+            recv_sem=self.recv_sems.at[slot],
+            device_id=self.sides[side][1],
+            device_id_type=MESH,
+        )
+
+    def start(self, side):
+        @pl.when(self.sides[side][0])
+        def _():
+            self.copy(side, side ^ 1).start()
+
+    def wait(self, side):
+        @pl.when(self.sides[side][0])
+        def _():
+            self.copy(side, side).wait_recv()
+
+        @pl.when(jnp.logical_not(self.sides[side][0]))
+        def _():
+            self.landing[side] = jnp.zeros_like(self.landing[side])
+
+    def finish(self):
+        for side in range(4):
+            @pl.when(self.sides[side][0])
+            def _():
+                self.copy(side, side).wait_send()
+
+
+def stack_rows(rows):
+    width = rows[0].shape[1]
+    place = lax.broadcasted_iota(jnp.int32, (8, width), 0)
+    out = jnp.zeros((8, width), jnp.float32)
+    for i, row in enumerate(rows):
+        out = jnp.where(place == i, row, out)
+    return out
+
+
+def send_edges(rim, fields):
+    last, right = fields[0].shape[0] - 1, fields[0].shape[1] - 1
+    rim.source[0] = stack_rows([f[0:1] for f in fields])
+    rim.start(0)
+    rim.source[1] = stack_rows([f[last:] for f in fields])
+    rim.start(1)
+    turned = [f.T for f in fields]
+    rim.source[2] = stack_rows([f[0:1] for f in turned])
+    rim.start(2)
+    rim.source[3] = stack_rows([f[right:] for f in turned])
+    rim.start(3)
+
+
+def rim_values(rim, count, shape):
+    for side in range(4):
+        rim.wait(side)
+    row_count, col_count = shape
+    line = lax.broadcasted_iota(jnp.int32, (col_count, row_count), 0)
+    result = []
+    for i in range(count):
+        low, high = rim.landing[0, i : i + 1], rim.landing[1, i : i + 1]
+        west, east = rim.landing[2, i : i + 1], rim.landing[3, i : i + 1]
+        side = jnp.where(line == 0, west, jnp.where(line == col_count - 1, east, 0.0)).T
+        result.append((low, high, side))
+    return result
+
+
+def around(field, rim):
+    low, high, side = rim
+    row_count, col_count = field.shape
+    row = lax.broadcasted_iota(jnp.int32, field.shape, 0)
+    col = lax.broadcasted_iota(jnp.int32, field.shape, 1)
+    return (
+        jnp.where(row == row_count - 1, high, pltpu.roll(field, row_count - 1, 0)),
+        jnp.where(row == 0, low, pltpu.roll(field, 1, 0)),
+        jnp.where(col == col_count - 1, side, pltpu.roll(field, col_count - 1, 1)),
+        jnp.where(col == 0, side, pltpu.roll(field, 1, 1)),
+    )
+
+
+def ice_kernel(
+    melt_ref,
+    node_ref,
+    thick_ref,
+    visc_ref,
+    fric_ref,
+    ground_ref,
+    coup_ref,
+    drive_ref,
+    guess_ref,
+    vel_ref,
+    res_ref,
+    melt_src,
+    melt_rows,
+    sum_src,
+    sum_rows,
+    half_src,
+    half_rows,
+    edge_src,
+    edge_land,
+    melt_send,
+    melt_recv,
+    sum_send,
+    sum_recv,
+    half_send,
+    half_recv,
+    edge_send,
+    edge_recv,
+):
+    tools = device_tools(("grp", "gx", "gy"))
+    grp, gx, gy, n_grp, n_gx, n_gy, sides = tools
+    enter(tools)
+    me = gx * n_gy + gy
+    peers = n_gx * n_gy
+    gather = Gather(tools, melt_src, melt_rows, melt_send, melt_recv)
+    gather.start(melt_ref[...])
+    shape = thick_ref.shape
+    width = melt_ref.shape[1]
+    node = node_ref[...]
+    friction = fric_ref[...] * ground_ref[...].astype(jnp.float32) + 0.2
+    cross = 0.9 * friction * coup_ref[...]
+    lane = lax.broadcasted_iota(jnp.int32, (1, width), 1)
+    row_of = (lax.broadcasted_iota(jnp.int32, (shape[0], width), 0) == jnp.where(node < 0, -1, node // shape[1])).astype(jnp.float32)
+    col_of = (lax.broadcasted_iota(jnp.int32, (shape[1], width), 0) == node % shape[1]).astype(jnp.float32)
+    gather.wait()
+    melt = jnp.zeros((1, width), jnp.float32)
+    for p in range(peers):
+        turn = lax.rem(CAP * (p - me) + width, width)
+        melt = jnp.where(lane // CAP == p, pltpu.roll(melt_rows[p], turn, 1), melt)
+    melt_node = lax.dot_general(
+        row_of * melt, col_of, (((1,), (1,)), ((), ())),
+        precision=lax.Precision.HIGHEST, preferred_element_type=jnp.float32,
+    )
+    thinned = thick_ref[...] * jnp.exp(-0.3 * melt_node)
+    depth_visc = visc_ref[...] * thinned
+    guess = [guess_ref[0], guess_ref[1]]
+    rims = [Rim(tools, edge_src.at[e], edge_land.at[e], edge_send.at[e], edge_recv.at[e]) for e in range(3)]
+    send_edges(rims[0], [depth_visc] + guess)
+    values = rim_values(rims[0], 3, shape)
+    weights = [0.5 * (depth_visc + beside) for beside in around(depth_visc, values[0])]
+    diagonal = weights[0] + weights[1] + weights[2] + weights[3] + friction
+    scale = 1.0 / diagonal
+
+    def apply(vector, rim):
+        out = []
+        for i in range(2):
+            beside = 0.0
+            for weight, side in zip(weights, around(vector[i], rim[i])):
+                beside = beside + weight * side
+            out.append(diagonal * vector[i] - beside + cross * vector[1 - i])
+        return out
+
+    def half_sums(index, products):
+        rows = [jnp.sum(a[0] * b[0] + a[1] * b[1], axis=0, keepdims=True) for a, b in products]
+        part = Gather(tools, sum_src.at[index], sum_rows.at[index], sum_send.at[index], sum_recv.at[index])
+        part.start(stack_rows(rows))
+        return part
+
+    def whole_sums(index, part, count):
+        part.wait()
+        total = jnp.sum(sum_rows[index], axis=0)
+        half_src[index] = total
+        copies = []
+        for i in range(1, n_grp):
+            copies.append(pltpu.make_async_remote_copy(
+                src_ref=half_src.at[index], dst_ref=half_rows.at[index, i - 1],
+                send_sem=half_send.at[index, i - 1], recv_sem=half_recv.at[index, i - 1],
+                device_id=(lax.rem(grp + i, n_grp), gx, gy), device_id_type=MESH,
+            ))
+            copies[-1].start()
+        for i, copy in enumerate(copies):
+            copy.wait()
+            total = total + half_rows[index, i]
+        summed = jnp.sum(total, axis=1, keepdims=True)
+        return [summed[i : i + 1] for i in range(count)]
+
+    image = apply(guess, values[1:])
+    residual = [drive_ref[i] * thinned - image[i] for i in range(2)]
+    precond = [residual[i] * scale for i in range(2)]
+    send_edges(rims[1], precond)
+    edge_z = rim_values(rims[1], 2, shape)
+    image = apply(precond, edge_z)
+    scaled = [image[i] * scale for i in range(2)]
+    part = half_sums(0, [(residual, precond), (precond, image)])
+    send_edges(rims[2], scaled)
+    edge_y = rim_values(rims[2], 2, shape)
+    norm, curve = whole_sums(0, part, 2)
+    step = norm / curve
+    velocity = [guess[i] + step * precond[i] for i in range(2)]
+    residual = [residual[i] - step * image[i] for i in range(2)]
+    next_precond = [residual[i] * scale for i in range(2)]
+    edge = [tuple(z - step * y for z, y in zip(edge_z[i], edge_y[i])) for i in range(2)]
+    next_image = apply(next_precond, edge)
+    second = half_sums(1, [(residual, next_precond), (next_precond, next_image), (next_precond, image)])
+    norm_next, own_curve, mixed = whole_sums(1, second, 3)
+    ratio = norm_next / norm
+    step = norm_next / (own_curve + 2.0 * ratio * mixed + ratio * ratio * curve)
+    for i in range(2):
+        vel_ref[i] = velocity[i] + step * (next_precond[i] + ratio * precond[i])
+        res_ref[i] = residual[i] - step * (next_image[i] + ratio * image[i])
+    gather.finish()
+    part.finish()
+    second.finish()
+    for rim in rims:
+        rim.finish()
+
+
+def ice_phase(melt_row, node_row, thickness, viscosity, friction, grounded, coupling, driving, first_guess):
+    n_grp, n_gx, n_gy = lax.axis_size("grp"), lax.axis_size("gx"), lax.axis_size("gy")
+    peers = n_gx * n_gy
+    width = melt_row.shape[1]
+    cols = thickness.shape[1]
+    vmem = pl.BlockSpec(memory_space=pltpu.VMEM)
+    dma = pltpu.SemaphoreType.DMA
+    f32 = jnp.float32
+    return pl.pallas_call(
+        ice_kernel,
+        out_shape=[jax.ShapeDtypeStruct(first_guess.shape, f32)] * 2,
+        in_specs=[vmem] * 9,
+        out_specs=[vmem] * 2,
+        scratch_shapes=[
+            pltpu.VMEM((1, width), f32),
+            pltpu.VMEM((peers, 1, width), f32),
+            pltpu.VMEM((2, 8, cols), f32),
+            pltpu.VMEM((2, peers, 8, cols), f32),
+            pltpu.VMEM((2, 8, cols), f32),
+            pltpu.VMEM((2, n_grp - 1, 8, cols), f32),
+            pltpu.VMEM((3, 4, 8, cols), f32),
+            pltpu.VMEM((3, 4, 8, cols), f32),
+            dma((peers,)),
+            dma((peers,)),
+            dma((2, peers)),
+            dma((2, peers)),
+            dma((2, n_grp - 1)),
+            dma((2, n_grp - 1)),
+            dma((3, 4)),
+            dma((3, 4)),
+        ],
+        compiler_params=pltpu.CompilerParams(
+            collective_id=0, has_side_effects=True, vmem_limit_bytes=32 * 1024 * 1024
+        ),
+    )(melt_row, node_row, thickness, viscosity, friction, grounded, coupling, driving, first_guess)
 
 
 def shards(
@@ -148,34 +468,21 @@
         total = total + melt_rate[margin : margin + row_count, margin : margin + col_count]
     fields = current
     melt_mean = total / NSUB
-    melt_item = melt_mean.reshape(-1)[columns]
-    melt_send = jnp.zeros((owner.size,), jnp.float32).at[slots].set(melt_item).reshape(owner.shape)
-    melt_recv = lax.all_to_all(melt_send, ("gx", "gy"), split_axis=0, concat_axis=0, tiled=True)
-    melt_node = (
-        jnp.zeros((thick_flat.shape[0],), jnp.float32)
-        .at[safe_node.reshape(-1)]
-        .add(melt_recv.reshape(-1))
-    )
-    thinned = thickness * jnp.exp(-0.3 * melt_node.reshape(thickness.shape))
-    depth_visc = viscosity * thinned
-    padded_first = ice_rim(jnp.concatenate([depth_visc[None], first_guess], 0))
-    parts = operator_parts(depth_visc, padded_first[0], friction, grounded, coupling)
-    rhs = driving * thinned
-    velocity = first_guess
-    residual = rhs - apply_padded(padded_first[1:], parts)
-    precond = residual / parts[0]
-    norm_now = ice_sum(jnp.sum(residual * precond))
-    direction = precond
-    for iteration in range(ITERS):
-        image = apply_padded(ice_rim(direction), parts)
-        step_size = norm_now / ice_sum(jnp.sum(direction * image))
-        velocity = velocity + step_size * direction
-        residual = residual - step_size * image
-        if iteration + 1 < ITERS:
-            precond = residual / parts[0]
-            norm_next = ice_sum(jnp.sum(residual * precond))
-            direction = precond + norm_next / norm_now * direction
-            norm_now = norm_next
+    lanes = 128 * (-(-owner.size // 128))
+    cells = jnp.arange(cell_count, dtype=jnp.int32)
+    melt_item = jnp.sum(
+        jnp.where(columns[:, None] == cells[None, :], melt_mean.reshape(1, -1), 0.0), axis=1
+    )
+    melt_row = jnp.sum(
+        jnp.where(
+            slots[:, None] == jnp.arange(lanes, dtype=jnp.int32)[None, :], melt_item[:, None], 0.0
+        ),
+        axis=0,
+    )[None]
+    node_row = jnp.pad(owner.reshape(1, -1), ((0, 0), (0, lanes - owner.size)), constant_values=-1)
+    velocity, residual = ice_phase(
+        melt_row, node_row, thickness, viscosity, friction, grounded, coupling, driving, first_guess
+    )
     return (fields, melt_mean, velocity, residual)
 
 

time: 294 us -> 117 us (0.40)
  blocking collectives: 125 us -> 0 us
  starting transfers between devices: 47.8 us -> 16.5 us
  Pallas kernels: 0 us -> 28 us
  waiting for transfers between devices: 54 us -> 26.7 us
  other arithmetic: 37.5 us -> 22.1 us
  between operations: 5.47 us -> 1.29 us
    psum x3 -> x0, blocking collectives: 125 us -> none  [ice_sum(): return lax.psum(value, ('grp', 'gx', 'gy'))]
    pallas_call x0 -> x1, Pallas kernels: none -> 28 us  [ice_phase(): pl.pallas_call(ice_kernel, out_shape=[jax.ShapeDtypeStruct(first_guess.sh...]
    ppermute x8 -> x2, starting transfers between devices: 25.7 us -> 5.59 us  [padded_2(): lax.ppermute(lax.slice_in_dim(block, block.shape[dim] - width, None, axis...]
    ppermute x8 -> x2, waiting for transfers between devices: 25.4 us -> 9.84 us  [padded_2(): lax.ppermute(lax.slice_in_dim(block, 0, width, axis=dim), axis, backward)]
    ppermute x8 -> x2, starting transfers between devices: 10.3 us -> 2.57 us  [padded_2(): lax.ppermute(lax.slice_in_dim(block, 0, width, axis=dim), axis, backward)]
    all_to_all x1 -> x0, waiting for transfers between devices: 7.15 us -> none  [shards(): lax.all_to_all(melt_send, ('gx', 'gy'), split_axis=0, concat_axis=0, tile...]
    add x4, other arithmetic: 19.9 us -> 14 us  [advance(): updated = fields + flux_sum]
    ppermute x8 -> x2, waiting for transfers between devices: 15.1 us -> 10.5 us  [padded_2(): lax.ppermute(lax.slice_in_dim(block, block.shape[dim] - width, None, axis...]
  transfers between devices with their start and end apart: 18 -> 5, of which waited for: 13 -> 4; matrix products, arithmetic and copies ran while one was open for 4% -> 4% of each run, Pallas kernels for 0% -> 0%
where the time goes in v1:
time: 117 us; the launch traced here: 116 us
  Pallas kernels  28 us (24%)
  waiting for transfers between devices  26.7 us (23%)
  other arithmetic  22.1 us (19%)
  local copies, waits for them, and re-layouts  21.5 us (18%)
  starting transfers between devices  16.5 us (14%)
  between operations  1.29 us (1%)
    pallas_call x1, Pallas kernels, ice_phase(): pl.pallas_call(ice_kernel, out_shape=[jax.ShapeDtypeStruct(first_guess.sh...  28 us
    add x4, other arithmetic, advance(): updated = fields + flux_sum  14 us
    ppermute x2, waiting for transfers between devices, padded_2(): lax.ppermute(lax.slice_in_dim(block, block.shape[dim] - width, None, axis...  10.5 us
    ppermute x2, waiting for transfers between devices, padded_2(): lax.ppermute(lax.slice_in_dim(block, 0, width, axis=dim), axis, backward)  9.84 us
    all_to_all x1, starting transfers between devices, shards(): lax.all_to_all(draft_send, ('gx', 'gy'), split_axis=0, concat_axis=0, til...  8.31 us
    all_to_all x1, waiting for transfers between devices, shards(): lax.all_to_all(draft_send, ('gx', 'gy'), split_axis=0, concat_axis=0, til...  6.3 us
    ppermute x2, starting transfers between devices, padded_2(): lax.ppermute(lax.slice_in_dim(block, block.shape[dim] - width, None, axis...  5.59 us
    slice x3, local copies, waits for them, and re-layouts, padded_2(): lax.slice_in_dim(block, block.shape[dim] - width, None, axis=dim)  5.19 us
  transfers between devices with their start and end apart: 5, of which 4 were waited for; matrix products, arithmetic and copies ran while one was open for 4% of the time, Pallas kernels for 0%

profile of v1, /device:TPU:0, one launch (start us, length us, event | category | flops | bytes accessed | tf_op | source)
XLA Modules:
  0.0 116.1 jit_solution(6180416286726480113)
XLA Ops:
  0.6 0.7 compare_select_fusion
  1.3 0.1 copy.72
  1.4 0.1 reshape.716
  1.5 0.0 copy-start.12
  1.6 1.7 %gather_fusion = f32[64]{0:T(128)S(1)} fusion(f32[16384]{0:T(1024)} %bitcast.389, s32[1024]{0:T(1024)S(1)} %pad_clamp_fusion.1), kind=kCustom, calls=%fused_computation | custom fusion | bytes 768 | tf_op jit(solution)/shard_map/gather | solution.py:429
  3.3 0.1 mul.837
  3.4 0.1 copy.73
  3.5 0.7 copy.74
  4.2 8.3 %all-to-all-start = ((f32[16,1,4]{2,1,0:T(1,128)}), f32[16,1,4]{2,1,0:T(1,128)S(1)}, u32[]{:S(2)}, u32[]{:S(2)}) async-start(f32[16,1,4]{2,1,0:T(1,128)} %copy.74), calls=%async_computation | async-start | bytes 16384 | tf_op jit(solution)/shard_map/all_to_all | solution.py:430
  12.5 0.1 constant_dynamic-update-slice_fusion.4
  12.7 0.7 scatter_custom_fusion
  13.4 6.3 %all-to-all-done = f32[16,1,4]{2,1,0:T(1,128)S(1)} async-done(((f32[16,1,4]{2,1,0:T(1,128)}), f32[16,1,4]{2,1,0:T(1,128)S(1)}, u32[]{:S(2)}, u32[]{:S(2)}) %all-to-all-start) | async-done | bytes 288 | tf_op jit(solution)/shard_map/all_to_all | solution.py:430
  19.7 0.5 broadcast.557
  20.2 0.7 reduce.11
  20.9 0.1 reshape.708
  20.9 0.7 gather_fusion.1
  21.6 0.7 scatter_custom_fusion.1
  22.4 0.2 fusion.140
  22.5 2.5 %collective-permute-start = (f32[244,4,128]{2,1,0:T(4,128)S(1)}, f32[244,4,128]{2,1,0:T(4,128)S(1)}, u32[]{:S(2)}, u32[]{:S(2)}) collective-permute-start(f32[244,4,128]{2,1,0:T(4,128)S(1)} %get-tuple-element.104), channel_id=1, source_target_pairs={{0,4},{4,8},{8,12},{12,16},{16,20},{20,24},{24,28},{1,5},{5,9},{9,... | collective-permute-start | bytes 1499144 | tf_op jit(solution)/shard_map/ppermute | solution.py:18
  25.0 1.3 %collective-permute-start.1 = (f32[244,4,128]{2,1,0:T(4,128)S(1)}, f32[244,4,128]{2,1,0:T(4,128)S(1)}, u32[]{:S(2)}, u32[]{:S(2)}) collective-permute-start(f32[244,4,128]{2,1,0:T(4,128)S(1)} %get-tuple-element.105), channel_id=1, source_target_pairs={{4,0},{8,4},{12,8},{16,12},{20,16},{24,20},{28,24},{5,1},{9,5},{13... | collective-permute-start | bytes 1499144 | tf_op jit(solution)/shard_map/ppermute | solution.py:21
  26.3 10.5 %collective-permute-done = f32[244,4,128]{2,1,0:T(4,128)S(1)} collective-permute-done((f32[244,4,128]{2,1,0:T(4,128)S(1)}, f32[244,4,128]{2,1,0:T(4,128)S(1)}, u32[]{:S(2)}, u32[]{:S(2)}) %collective-permute-start) | collective-permute-done | bytes 499744 | tf_op jit(solution)/shard_map/ppermute | solution.py:18
  36.8 6.8 %collective-permute-done.1 = f32[244,4,128]{2,1,0:T(4,128)S(1)} collective-permute-done((f32[244,4,128]{2,1,0:T(4,128)S(1)}, f32[244,4,128]{2,1,0:T(4,128)S(1)}, u32[]{:S(2)}, u32[]{:S(2)}) %collective-permute-start.1) | collective-permute-done | bytes 499744 | tf_op jit(solution)/shard_map/ppermute | solution.py:21
  43.7 0.8 copy-done.8
  44.5 0.4 pad_maximum_fusion.1
  44.8 1.9 %fusion.139 = (f32[244,16,4]{2,1,0:T(8,128)}, f32[244,16,4]{2,1,0:T(8,128)S(1)}) fusion(f32[244,16,128]{2,1,0:T(8,128)S(1)} %pad_maximum_fusion.1), kind=kLoop, calls=%fused_computation.297 | loop fusion | bytes 249856 | tf_op jit(solution)/shard_map/slice | solution.py:19
  46.8 3.1 %copy.75 = f32[244,16,4]{0,1,2:T(8,128)} copy(f32[244,16,4]{2,1,0:T(8,128)} %get-tuple-element.100) | data formatting | bytes 124928 | tf_op jit(solution)/shard_map/slice | solution.py:19
  49.9 3.1 %collective-permute-start.2 = (f32[244,16,4]{0,1,2:T(8,128)}, f32[244,16,4]{0,1,2:T(8,128)}, u32[]{:S(2)}, u32[]{:S(2)}) collective-permute-start(f32[244,16,4]{0,1,2:T(8,128)} %copy.75), channel_id=1, source_target_pairs={{0,1},{1,2},{2,3},{4,5},{5,6},{6,7},{8,9},{9,10},{10,11},{12,13},{... | collective-permute-start | bytes 187400 | tf_op jit(solution)/shard_map/ppermute | solution.py:18
  52.9 1.7 %copy.76 = f32[244,16,4]{0,1,2:T(8,128)} copy(f32[244,16,4]{2,1,0:T(8,128)S(1)} %get-tuple-element.101) | data formatting | bytes 124928 | tf_op jit(solution)/shard_map/slice | solution.py:21
  54.6 1.3 %collective-permute-start.3 = (f32[244,16,4]{0,1,2:T(8,128)}, f32[244,16,4]{0,1,2:T(8,128)}, u32[]{:S(2)}, u32[]{:S(2)}) collective-permute-start(f32[244,16,4]{0,1,2:T(8,128)} %copy.76), channel_id=1, source_target_pairs={{1,0},{2,1},{3,2},{5,4},{6,5},{7,6},{9,8},{10,9},{11,10},{13,12},{... | collective-permute-start | bytes 187400 | tf_op jit(solution)/shard_map/ppermute | solution.py:21
  55.9 0.1 copy.86
  56.0 0.1 reshape_squeeze.3
  56.1 2.0 %copy.77 = f32[244,16,4]{2,1,0:T(8,128)S(1)} copy(f32[244,16,4]{0,1,2:T(8,128)} %collective-permute-done.2) | data formatting | bytes 124928 | tf_op jit(solution)/shard_map/ppermute | solution.py:18
  58.1 3.0 %collective-permute-done.3 = f32[244,16,4]{0,1,2:T(8,128)} collective-permute-done((f32[244,16,4]{0,1,2:T(8,128)}, f32[244,16,4]{0,1,2:T(8,128)}, u32[]{:S(2)}, u32[]{:S(2)}) %collective-permute-start.3) | collective-permute-done | bytes 62496 | tf_op jit(solution)/shard_map/ppermute | solution.py:21
  61.1 3.2 %copy.78 = f32[244,16,4]{2,1,0:T(8,128)} copy(f32[244,16,4]{0,1,2:T(8,128)} %collective-permute-done.3) | data formatting | bytes 124928 | tf_op jit(solution)/shard_map/ppermute | solution.py:21
  64.3 4.4 %pad_maximum_fusion = f32[244,16,136]{2,1,0:T(8,128)S(1)} fusion(f32[244,16,4]{2,1,0:T(8,128)} %copy.78, f32[244,4,128]{2,1,0:T(4,128)} %copy-done.8, f32[244,8,128]{2,1,0:T(8,128)S(1)} %constant_dynamic-update-slice_fusion, f32[244,4,128]{2,1,0:T(4,128)S(1)} %collective-permute-done, f32[244,16,4]{2,1,0:T(8,128)S(1)} %copy.77), kind=kLoop, calls=%fused_computation.4 | loop fusion | flops 2123776 | bytes 4247552 | tf_op jit(solution)/shard_map/concatenate | solution.py:22
  68.8 0.4 slice.592
  69.2 0.1 fusion.94
  69.3 1.0 copy-done.7
  70.3 0.1 copy-done.9
  70.4 0.1 maximum_bitcast_fusion.8
  70.5 0.1 slice_multiply_fusion.14
  70.6 4.4 %fusion.18 = f32[4,60,14,134]{3,2,1,0:T(8,128)S(1)} fusion(f32[4,60,16,136]{3,2,1,0:T(8,128)S(1)} %bitcast.392, f32[14,134]{1,0:T(8,128)S(1)} %get-tuple-element.130, f32[14,134]{1,0:T(8,128)S(1)} %get-tuple-element.128, f32[14,134]{1,0:T(8,128)S(1)} %get-tuple-element.129, f32[14,134]{1,0:T(8,128)S(1)} %get-tuple-element.127), kind=kLoop, calls=%fused_computation.32 | loop fusion | flops 5402880 | bytes 10835776 | tf_op jit(solution)/shard_map/add | solution.py:48
  75.0 0.1 maximum_bitcast_fusion.6
  75.1 0.1 fusion.63
  75.3 0.1 slice_bitcast_fusion.13
  75.4 0.1 fusion.95
  75.4 0.1 slice_multiply_fusion.9
  75.6 4.2 %fusion.10 = f32[4,60,12,132]{3,2,1,0:T(8,128)S(1)} fusion(f32[4,60,14,134]{3,2,1,0:T(8,128)S(1)} %constant_dynamic-update-slice_fusion.7, f32[12,132]{1,0:T(8,128)S(1)} %get-tuple-element.126, f32[12,132]{1,0:T(8,128)S(1)} %get-tuple-element.124, f32[12,132]{1,0:T(8,128)S(1)} %get-tuple-element.125, f32[12,132]{1,0:T(8,128)S(1)} %get-tuple-element.123), kind=kLoop, calls=%fused_computation.20 | loop fusion | flops 4561920 | bytes 9149184 | tf_op jit(solution)/shard_map/add | solution.py:48
  79.8 0.1 maximum_bitcast_fusion.4
  79.9 0.1 fusion.51
  80.1 0.1 fusion.96
  80.2 0.1 slice_multiply_fusion.4
  80.3 4.2 %fusion.2 = f32[4,60,10,130]{3,2,1,0:T(8,128)S(1)} fusion(f32[4,60,12,132]{3,2,1,0:T(8,128)S(1)} %constant_dynamic-update-slice_fusion.6, f32[10,130]{1,0:T(8,128)S(1)} %get-tuple-element.122, f32[10,130]{1,0:T(8,128)S(1)} %get-tuple-element.120, f32[10,130]{1,0:T(8,128)S(1)} %get-tuple-element.121, f32[10,130]{1,0:T(8,128)S(1)} %get-tuple-element.119), kind=kLoop, calls=%fused_computation.8 | loop fusion | flops 3744000 | bytes 7508800 | tf_op jit(solution)/shard_map/add | solution.py:48
  84.5 0.1 maximum_bitcast_fusion.2
  84.6 0.1 fusion.39
  84.9 0.1 slice_multiply_fusion.25
  85.0 1.1 fusion.26
  86.1 0.1 fusion.107
  86.2 0.1 fusion.99
  86.3 0.2 select_reduce_fusion
  86.5 0.1 select_reduce_fusion.1
  86.7 28.0 %shard_map.156 = (f32[2,128,128]{2,1,0:T(8,128)S(1)}, f32[2,128,128]{2,1,0:T(8,128)S(1)}) custom-call(f32[1,128]{1,0:T(1,128)S(1)} %bitcast.390, s32[1,128]{1,0:T(1,128)S(1)} %pad.12.node_ref, f32[128,128]{1,0:T(8,128)S(1)} %copy-done, f32[128,128]{1,0:T(8,128)S(1)} %copy-done.3, f32[128,128]{1,0:T(8,128)S(1)} %copy-done.4, s32[128,128]{1,0:T(8,128)S(1)} %copy-done.5, ...), custom_call_target="tpu_custom_call" | custom-call | tf_op jit(solution)/shard_map/pallas_call | solution.py:379
  114.7 0.7 copy.97
  115.4 0.7 copy.98
  (56 shorter events, 0.3 us)
Async XLA Ops:
  1.5 1.9 %copy-start.12 = (s32[1,1,16,4]{2,3,1,0:T(4,128)S(1)}, s32[1,1,16,4]{2,3,1,0:T(4,128)}, u32[]{:S(2)}) copy-start(s32[1,1,16,4]{2,3,1,0:T(4,128)} %param.26) | copy-start | bytes 772
  1.5 11.0 %copy-start.16 = (s32[1,1,32]{2,1,0:T(1,128)S(1)}, s32[1,1,32]{2,1,0:T(1,128)}, u32[]{:S(2)}) copy-start(s32[1,1,32]{2,1,0:T(1,128)} %param.24) | copy-start | bytes 388
  1.5 11.0 %copy-start.17 = (s32[1,1,32]{2,1,0:T(1,128)S(1)}, s32[1,1,32]{2,1,0:T(1,128)}, u32[]{:S(2)}) copy-start(s32[1,1,32]{2,1,0:T(1,128)} %param.25) | copy-start | bytes 388
  1.5 11.0 %copy-start.11 = (f32[4,60,8,128]{3,2,1,0:T(8,128)S(1)}, f32[4,60,8,128]{3,2,1,0:T(8,128)}, u32[]{:S(2)}) copy-start(f32[4,60,8,128]{3,2,1,0:T(8,128)} %param.21) | copy-start | bytes 2949124
  1.6 11.1 %copy-start.14 = (f32[8,128]{1,0:T(8,128)S(1)}, f32[8,128]{1,0:T(8,128)}, u32[]{:S(2)}) copy-start(f32[8,128]{1,0:T(8,128)} %param.22) | copy-start | bytes 12292
  1.6 11.1 %copy-start.15 = (s32[8,128]{1,0:T(8,128)S(1)}, s32[8,128]{1,0:T(8,128)}, u32[]{:S(2)}) copy-start(s32[8,128]{1,0:T(8,128)} %param.23) | copy-start | bytes 12292
  4.2 15.5 %all-to-all-start = ((f32[16,1,4]{2,1,0:T(1,128)}), f32[16,1,4]{2,1,0:T(1,128)S(1)}, u32[]{:S(2)}, u32[]{:S(2)}) async-start(f32[16,1,4]{2,1,0:T(1,128)} %copy.74), calls=%async_computation | async-start | bytes 16384 | tf_op jit(solution)/shard_map/all_to_all | solution.py:430
  22.5 14.3 %collective-permute-start = (f32[244,4,128]{2,1,0:T(4,128)S(1)}, f32[244,4,128]{2,1,0:T(4,128)S(1)}, u32[]{:S(2)}, u32[]{:S(2)}) collective-permute-start(f32[244,4,128]{2,1,0:T(4,128)S(1)} %get-tuple-element.104), channel_id=1, source_target_pairs={{0,4},{4,8},{8,12},{12,16},{16,20},{20,24},{24,28},{1,5},{5,9},{9,... | collective-permute-start | bytes 1499144 | tf_op jit(solution)/shard_map/ppermute | solution.py:18
  25.0 18.6 %collective-permute-start.1 = (f32[244,4,128]{2,1,0:T(4,128)S(1)}, f32[244,4,128]{2,1,0:T(4,128)S(1)}, u32[]{:S(2)}, u32[]{:S(2)}) collective-permute-start(f32[244,4,128]{2,1,0:T(4,128)S(1)} %get-tuple-element.105), channel_id=1, source_target_pairs={{4,0},{8,4},{12,8},{16,12},{20,16},{24,20},{28,24},{5,1},{9,5},{13... | collective-permute-start | bytes 1499144 | tf_op jit(solution)/shard_map/ppermute | solution.py:21
  43.7 0.8 copy-start.8
  49.9 6.3 %collective-permute-start.2 = (f32[244,16,4]{0,1,2:T(8,128)}, f32[244,16,4]{0,1,2:T(8,128)}, u32[]{:S(2)}, u32[]{:S(2)}) collective-permute-start(f32[244,16,4]{0,1,2:T(8,128)} %copy.75), channel_id=1, source_target_pairs={{0,1},{1,2},{2,3},{4,5},{5,6},{6,7},{8,9},{9,10},{10,11},{12,13},{... | collective-permute-start | bytes 187400 | tf_op jit(solution)/shard_map/ppermute | solution.py:18
  54.6 6.5 %collective-permute-start.3 = (f32[244,16,4]{0,1,2:T(8,128)}, f32[244,16,4]{0,1,2:T(8,128)}, u32[]{:S(2)}, u32[]{:S(2)}) collective-permute-start(f32[244,16,4]{0,1,2:T(8,128)} %copy.76), channel_id=1, source_target_pairs={{1,0},{2,1},{3,2},{5,4},{6,5},{7,6},{9,8},{10,9},{11,10},{13,12},{... | collective-permute-start | bytes 187400 | tf_op jit(solution)/shard_map/ppermute | solution.py:21
  68.7 1.6 %copy-start.7 = (f32[244,16,4]{2,1,0:T(8,128)S(1)}, f32[244,16,4]{2,1,0:T(8,128)}, u32[]{:S(2)}) copy-start(f32[244,16,4]{2,1,0:T(8,128)} %copy.78) | copy-start | bytes 187396
  68.7 1.6 %copy-start.9 = (f32[244,4,128]{2,1,0:T(4,128)S(1)}, f32[244,4,128]{2,1,0:T(4,128)}, u32[]{:S(2)}) copy-start(f32[244,4,128]{2,1,0:T(4,128)} %copy-done.8) | copy-start | bytes 1499140
  84.8 1.8 %copy-start = (f32[128,128]{1,0:T(8,128)S(1)}, f32[128,128]{1,0:T(8,128)}, u32[]{:S(2)}) copy-start(f32[128,128]{1,0:T(8,128)} %thick_ref.1) | copy-start | bytes 196612
  84.8 1.8 %copy-start.1 = (f32[2,128,128]{2,1,0:T(8,128)S(1)}, f32[2,128,128]{2,1,0:T(8,128)}, u32[]{:S(2)}) copy-start(f32[2,128,128]{2,1,0:T(8,128)} %drive_ref.1) | copy-start | bytes 393220
  84.8 1.8 %copy-start.2 = (f32[2,128,128]{2,1,0:T(8,128)S(1)}, f32[2,128,128]{2,1,0:T(8,128)}, u32[]{:S(2)}) copy-start(f32[2,128,128]{2,1,0:T(8,128)} %guess_ref.1) | copy-start | bytes 393220
  84.8 1.8 %copy-start.3 = (f32[128,128]{1,0:T(8,128)S(1)}, f32[128,128]{1,0:T(8,128)}, u32[]{:S(2)}) copy-start(f32[128,128]{1,0:T(8,128)} %visc_ref.1) | copy-start | bytes 196612
  84.8 1.8 %copy-start.4 = (f32[128,128]{1,0:T(8,128)S(1)}, f32[128,128]{1,0:T(8,128)}, u32[]{:S(2)}) copy-start(f32[128,128]{1,0:T(8,128)} %fric_ref.1) | copy-start | bytes 196612
  84.8 1.8 %copy-start.5 = (s32[128,128]{1,0:T(8,128)S(1)}, s32[128,128]{1,0:T(8,128)}, u32[]{:S(2)}) copy-start(s32[128,128]{1,0:T(8,128)} %ground_ref.1) | copy-start | bytes 196612
  84.8 1.8 %copy-start.6 = (f32[128,128]{1,0:T(8,128)S(1)}, f32[128,128]{1,0:T(8,128)}, u32[]{:S(2)}) copy-start(f32[128,128]{1,0:T(8,128)} %coup_ref.1) | copy-start | bytes 196612
  86.3 29.8 %copy-start.13 = (f32[8,128]{1,0:T(8,128)}, f32[8,128]{1,0:T(8,128)S(1)}, u32[]{:S(2)}) copy-start(f32[8,128]{1,0:T(8,128)S(1)} %fusion.99) | copy-start | bytes 12292
  114.7 1.4 %copy-start.10 = (f32[4,60,8,128]{3,2,1,0:T(8,128)}, f32[4,60,8,128]{3,2,1,0:T(8,128)S(1)}, u32[]{:S(2)}) copy-start(f32[4,60,8,128]{3,2,1,0:T(8,128)S(1)} %fusion.72) | copy-start | bytes 2949124

commit v2 on v1

--- a/solution.py
+++ b/solution.py
@@ -1,3 +1,5 @@
+import functools
+
 import jax
 import jax.numpy as jnp
 from jax import lax
@@ -8,55 +10,6 @@
 NSUB = 4
 CAP = 4
 MESH = pl.DeviceIdType.MESH
-
-
-def padded_2(block, sides, width):
-    for axis, dim in sides:
-        count = lax.axis_size(axis)
-        forward = [(i, i + 1) for i in range(count - 1)]
-        backward = [(target, source) for source, target in forward]
-        low = lax.ppermute(
-            lax.slice_in_dim(block, block.shape[dim] - width, None, axis=dim), axis, forward
-        )
-        high = lax.ppermute(lax.slice_in_dim(block, 0, width, axis=dim), axis, backward)
-        block = jnp.concatenate([low, block, high], axis=dim)
-    return block
-
-
-def advance(padded, diff_pad, wet_pad, cover, draft_field):
-    fields = padded[:, :, 1:-1, 1:-1]
-    row_total = fields.shape[2]
-    col_total = fields.shape[3]
-    diff_here = diff_pad[1:-1, 1:-1]
-    wet_here = wet_pad[1:-1, 1:-1]
-    flux_sum = jnp.zeros_like(fields)
-    for offset in ((2, 1), (0, 1), (1, 2), (1, 0)):
-        diff_side = diff_pad[offset[0] : offset[0] + row_total, offset[1] : offset[1] + col_total]
-        wet_side = wet_pad[offset[0] : offset[0] + row_total, offset[1] : offset[1] + col_total]
-        side_vals = padded[
-            :, :, offset[0] : offset[0] + row_total, offset[1] : offset[1] + col_total
-        ]
-        weight = 0.5 * (diff_here + diff_side) * wet_here * wet_side
-        flux_sum = flux_sum + weight * (side_vals - fields)
-    top_temp = fields[0, 0]
-    top_salt = fields[1, 0]
-    top_east = fields[2, 0]
-    top_north = fields[3, 0]
-    current_speed = jnp.sqrt(top_east * top_east + top_north * top_north + 0.01)
-    freezing = -0.5 * top_salt + 0.3 * draft_field - 0.2
-    melt_rate = 0.5 * cover * (top_temp - freezing) * current_speed
-    updated = fields + flux_sum
-    drag_rate = 0.05 * cover * current_speed
-    top_rows = jnp.stack(
-        [
-            updated[0, 0] - 0.3 * melt_rate,
-            updated[1, 0] - 0.2 * melt_rate,
-            updated[2, 0] - drag_rate * top_east,
-            updated[3, 0] - drag_rate * top_north,
-        ]
-    )
-    updated = updated.at[:, 0].set(top_rows)
-    return (updated, melt_rate)
 
 
 def device_tools(names):
@@ -241,8 +194,338 @@
     )
 
 
-def ice_kernel(
-    melt_ref,
+def dot(a, b, a_dim, b_dim):
+    return lax.dot_general(
+        a, b, (((a_dim,), (b_dim,)), ((), ())),
+        precision=lax.Precision.HIGHEST, preferred_element_type=jnp.float32,
+    )
+
+
+class Edge:
+    def __init__(self, tools, first, sources, landings, send_sems, recv_sems):
+        self.sides = tools[6][first : first + 2]
+        self.sources, self.landings = sources, landings
+        self.send_sems, self.recv_sems = send_sems, recv_sems
+
+    def copy(self, side, slot):
+        return pltpu.make_async_remote_copy(
+            src_ref=self.sources[side],
+            dst_ref=self.landings[slot],
+            send_sem=self.send_sems.at[side],
+            recv_sem=self.recv_sems.at[slot],
+            device_id=self.sides[side][1],
+            device_id_type=MESH,
+        )
+
+    def start(self):
+        for side in range(2):
+            @pl.when(self.sides[side][0])
+            def _():
+                self.copy(side, 1 - side).start()
+
+    def wait(self):
+        for side in range(2):
+            @pl.when(self.sides[side][0])
+            def _():
+                self.copy(side, side).wait_recv()
+
+            @pl.when(jnp.logical_not(self.sides[side][0]))
+            def _():
+                self.landings[side][...] = jnp.zeros(self.landings[side].shape, jnp.float32)
+
+    def finish(self):
+        for side in range(2):
+            @pl.when(self.sides[side][0])
+            def _():
+                self.copy(side, side).wait_send()
+
+
+def row_tiles(layers):
+    half = len(layers) // 2
+    count = layers[0].shape[0]
+    row = lax.broadcasted_iota(jnp.int32, layers[0].shape, 0)
+    low, high = [], []
+    for a, b in zip(layers[:half], layers[half:]):
+        turned = pltpu.roll(b, count // 2, 0)
+        low.append(jnp.where(row < count // 2, a, turned))
+        high.append(jnp.where(row < count // 2, turned, a))
+    return low, high
+
+
+def halo_tiles(from_low, from_high):
+    count = from_low[0].shape[0]
+    row = lax.broadcasted_iota(jnp.int32, from_low[0].shape, 0)
+    first, second = [], []
+    for low, high in zip(from_low, from_high):
+        first.append(jnp.where(row < count // 2, high, low))
+        second.append(pltpu.roll(jnp.where(row < count // 2, low, high), count // 2, 0))
+    return first + second
+
+
+def packed(layers):
+    lane = lax.broadcasted_iota(jnp.int32, layers[0].shape, 1)
+    out = jnp.zeros(layers[0].shape, jnp.float32)
+    for g, layer in enumerate(layers):
+        moved = pltpu.roll(layer, (2 * NSUB * g + NSUB) % layer.shape[1], 1)
+        out = jnp.where(lane // (2 * NSUB) == g, moved, out)
+    return out
+
+
+def joined(left, right):
+    lane = lax.broadcasted_iota(jnp.int32, left.shape, 1)
+    return jnp.where(lane % (2 * NSUB) < NSUB, left, right)
+
+
+def repeated(pack, slot):
+    group = 2 * NSUB
+    width = pack.shape[1]
+    lane = lax.broadcasted_iota(jnp.int32, pack.shape, 1)
+    out = jnp.where(lane // group == slot, pack, 0.0)
+    reach = group
+    while reach < width:
+        out = out + pltpu.roll(out, reach, 1)
+        reach *= 2
+    return out
+
+
+def row_ring(pair):
+    main, halo = pair
+    count = main.shape[0]
+    row = lax.broadcasted_iota(jnp.int32, main.shape, 0)
+    main_up, halo_up = pltpu.roll(main, count - 1, 0), pltpu.roll(halo, count - 1, 0)
+    main_down, halo_down = pltpu.roll(main, 1, 0), pltpu.roll(halo, 1, 0)
+    end, begin = row == count - 1, row == 0
+    return (
+        (jnp.where(end, halo_up, main_up), jnp.where(end, main_up, halo_up)),
+        (jnp.where(begin, halo_down, main_down), jnp.where(begin, main_down, halo_down)),
+    )
+
+
+def ring_sides(pair, west=None, east=None):
+    width = pair[0].shape[1]
+    lane = lax.broadcasted_iota(jnp.int32, pair[0].shape, 1)
+    up, down = row_ring(pair)
+    right = [pltpu.roll(x, width - 1, 1) for x in pair]
+    left = [pltpu.roll(x, 1, 1) for x in pair]
+    if west is not None:
+        right = [jnp.where(lane == width - 1, e, x) for e, x in zip(east, right)]
+        left = [jnp.where(lane == 0, w, x) for w, x in zip(west, left)]
+    return up, down, right, left
+
+
+def ring_weights(mix, wet, mix_ends=(None, None), wet_ends=(None, None)):
+    weights = []
+    for mix_side, wet_side in zip(ring_sides(mix, *mix_ends), ring_sides(wet, *wet_ends)):
+        weights.append([0.5 * (mix[t] + mix_side[t]) * wet[t] * wet_side[t] for t in range(2)])
+    stay = [1.0 - (weights[0][t] + weights[1][t] + weights[2][t] + weights[3][t]) for t in range(2)]
+    return weights, stay
+
+
+def spread(pair, weights, west=None, east=None, tiles=2):
+    sides, stay = ring_sides(pair, west, east), weights[1]
+    out = []
+    for t in range(tiles):
+        total = stay[t] * pair[t]
+        for weight, side in zip(weights[0], sides):
+            total = total + weight[t] * side[t]
+        out.append(total)
+    return out
+
+
+def column(pair, lane):
+    return [x[:, lane : lane + 1] for x in pair]
+
+
+def surface(fields, moved, cover, draft, tile):
+    temp, salt, east, north = [f[tile] for f in fields]
+    speed = jnp.sqrt(east * east + north * north + 0.01)
+    freezing = -0.5 * salt + 0.3 * draft[tile] - 0.2
+    melt = 0.5 * cover[tile] * (temp - freezing) * speed
+    drag = 0.05 * cover[tile] * speed
+    moved[0][tile] = moved[0][tile] - 0.3 * melt
+    moved[1][tile] = moved[1][tile] - 0.2 * melt
+    moved[2][tile] = moved[2][tile] - drag * east
+    moved[3][tile] = moved[3][tile] - drag * north
+    return melt
+
+
+def slot_table(rows, me, peers, width):
+    lane = lax.broadcasted_iota(jnp.int32, (1, width), 1)
+    out = jnp.zeros((1, width), jnp.float32)
+    for p in range(peers):
+        turn = lax.rem(CAP * (p - me) + width, width)
+        out = jnp.where(lane // CAP == p, pltpu.roll(rows[p], turn, 1), out)
+    return out
+
+
+def tall(row):
+    return jnp.broadcast_to(row, (8, row.shape[1]))
+
+
+class Ocean:
+    def __init__(self, tools, state_ref, next_ref, halo_ref, weight_ref, buffers):
+        self.tools, self.state, self.next = tools, state_ref, next_ref
+        self.halo, self.weight_ref = halo_ref, weight_ref
+        (row_src, row_land, col_src, col_land, row_send, row_recv, col_send, col_recv) = buffers
+        self.row_src, self.row_land = row_src, row_land
+        self.col_src, self.col_land = col_src, col_land
+        self.group = state_ref.shape[2] // (2 * NSUB)
+        self.packs = state_ref.shape[0] // self.group
+        self.chunks = max(c for c in range(1, 4) if self.packs % c == 0)
+        self.each = self.packs // self.chunks
+        half = self.group // 2
+        self.row_edges, self.col_edges = [], []
+        for c in range(self.chunks):
+            rows, cols = pl.ds(c * self.each * half, self.each * half), pl.ds(c * self.each, self.each)
+            self.row_edges.append(Edge(
+                tools, 0, [row_src.at[s, rows] for s in range(2)],
+                [row_land.at[s, rows] for s in range(2)], row_send.at[c], row_recv.at[c],
+            ))
+            self.col_edges.append(Edge(
+                tools, 2, [col_src.at[cols]] * 2,
+                [col_land.at[s, cols] for s in range(2)], col_send.at[c], col_recv.at[c],
+            ))
+
+    def loop(self, c, step):
+        def body(v, carry):
+            step(v)
+            return carry
+
+        lax.fori_loop(c * self.each, (c + 1) * self.each, body, 0)
+
+    def send_rows(self, c):
+        half = self.group // 2
+
+        def step(v):
+            layers = [self.state[v * self.group + j] for j in range(self.group)]
+            low, high = row_tiles(layers)
+            for j in range(half):
+                self.row_src[0, v * half + j] = low[j]
+                self.row_src[1, v * half + j] = high[j]
+
+        self.loop(c, step)
+        self.row_edges[c].start()
+
+    def send_columns(self, c):
+        half = self.group // 2
+        self.row_edges[c].wait()
+
+        def step(v):
+            low = [self.row_land[0, v * half + j] for j in range(half)]
+            high = [self.row_land[1, v * half + j] for j in range(half)]
+            halo = halo_tiles(low, high)
+            for j in range(self.group):
+                self.halo[v * self.group + j] = halo[j]
+            self.col_src[v, 0] = packed([self.state[v * self.group + j] for j in range(self.group)])
+            self.col_src[v, 1] = packed(halo)
+
+        self.loop(c, step)
+        self.col_edges[c].start()
+
+    def compute(self, c):
+        self.col_edges[c].wait()
+
+        def weights_of(block):
+            pick = [[self.weight_ref[block, k, t] for t in range(2)] for k in range(5)]
+            return pick[:4], pick[4]
+
+        def step(v):
+            wings = []
+            for block in (0, 2):
+                pair = []
+                for t in range(2):
+                    own = self.col_src[v, t]
+                    if block == 0:
+                        pair.append(joined(self.col_land[0, v, t], own))
+                    else:
+                        pair.append(joined(own, self.col_land[1, v, t]))
+                stages = [pair]
+                weights = weights_of(block)
+                for _ in range(NSUB - 1):
+                    stages.append(spread(stages[-1], weights))
+                wings.append(stages)
+            weights = weights_of(1)
+            for j in range(self.group):
+                place = 2 * NSUB * j
+                pair = [self.state[v * self.group + j], self.halo[v * self.group + j]]
+                for s in range(NSUB):
+                    west = column(wings[0][s], place + NSUB - 1)
+                    east = column(wings[1][s], place + NSUB)
+                    pair = spread(pair, weights, west, east, 1 if s == NSUB - 1 else 2)
+                self.next[v * self.group + j] = pair[0]
+
+        self.loop(c, step)
+
+    def finish(self):
+        for edge in self.row_edges + self.col_edges:
+            edge.finish()
+
+
+def top_exchange(tools, layers, src, land, send, recv):
+    half = len(layers) // 2
+    low, high = row_tiles(layers)
+    for j in range(half):
+        src[0, j] = low[j]
+        src[1, j] = high[j]
+    rows = Edge(tools, 0, [src.at[0], src.at[1]], [land.at[0], land.at[1]], send.at[0], recv.at[0])
+    rows.start()
+    rows.wait()
+    halo = halo_tiles([land[0, j] for j in range(half)], [land[1, j] for j in range(half)])
+    own = [packed(layers), packed(halo)]
+    src[2, 0], src[2, 1] = own
+    cols = Edge(
+        tools, 2, [src.at[2, pl.ds(0, 2)]] * 2, [land.at[2, pl.ds(0, 2)], land.at[3, pl.ds(0, 2)]],
+        send.at[1], recv.at[1],
+    )
+    cols.start()
+    cols.wait()
+    west = [joined(land[2, t], own[t]) for t in range(2)]
+    east = [joined(own[t], land[3, t]) for t in range(2)]
+    blocks = [[[repeated(x, i) for x in west] for i in range(len(layers))]]
+    blocks.append([[layers[i], halo[i]] for i in range(len(layers))])
+    blocks.append([[repeated(x, i) for x in east] for i in range(len(layers))])
+    return blocks, (rows, cols)
+
+
+def top_steps(blocks, weight_ref, levels, next_ref):
+    def ends(i):
+        return column(blocks[0][i], NSUB - 1), column(blocks[2][i], NSUB)
+
+    weights = [
+        ring_weights(blocks[0][4], blocks[0][5]),
+        ring_weights(blocks[1][4], blocks[1][5], ends(4), ends(5)),
+        ring_weights(blocks[2][4], blocks[2][5]),
+    ]
+    for b in range(3):
+        for t in range(2):
+            for k in range(4):
+                weight_ref[b, k, t] = weights[b][0][k][t]
+            weight_ref[b, 4, t] = weights[b][1][t]
+    fields = [block[:4] for block in blocks]
+    total = 0.0
+    for s in range(NSUB):
+        moved = [[], [], []]
+        for i in range(4):
+            moved[0].append(spread(fields[0][i], weights[0]))
+            west, east = column(fields[0][i], NSUB - 1), column(fields[2][i], NSUB)
+            moved[1].append(spread(fields[1][i], weights[1], west, east))
+            moved[2].append(spread(fields[2][i], weights[2]))
+        for b in range(3):
+            for t in range(2):
+                melt = surface(fields[b], moved[b], blocks[b][6], blocks[b][7], t)
+                if b == 1 and t == 0:
+                    total = total + melt
+        fields = moved
+    return [fields[1][i][0] for i in range(4)], total / NSUB
+
+
+def step_kernel(
+    levels,
+    state_ref,
+    mix_ref,
+    wet_ref,
+    cell_ref,
+    slot_ref,
     node_ref,
     thick_ref,
     visc_ref,
@@ -251,18 +534,34 @@
     coup_ref,
     drive_ref,
     guess_ref,
+    next_ref,
+    mean_ref,
     vel_ref,
     res_ref,
-    melt_src,
-    melt_rows,
+    halo_ref,
+    weight_ref,
+    row_src,
+    row_land,
+    col_src,
+    col_land,
+    top_src,
+    top_land,
+    list_src,
+    list_rows,
     sum_src,
     sum_rows,
     half_src,
     half_rows,
     edge_src,
     edge_land,
-    melt_send,
-    melt_recv,
+    row_send,
+    row_recv,
+    col_send,
+    col_recv,
+    top_send,
+    top_recv,
+    list_send,
+    list_recv,
     sum_send,
     sum_recv,
     half_send,
@@ -275,30 +574,58 @@
     enter(tools)
     me = gx * n_gy + gy
     peers = n_gx * n_gy
-    gather = Gather(tools, melt_src, melt_rows, melt_send, melt_recv)
-    gather.start(melt_ref[...])
     shape = thick_ref.shape
-    width = melt_ref.shape[1]
-    node = node_ref[...]
+    width = node_ref.shape[1]
+    items = cell_ref.shape[1]
+    node, cell = node_ref[...], cell_ref[...]
+    gathers = [
+        Gather(tools, list_src.at[e], list_rows.at[e], list_send.at[e], list_recv.at[e])
+        for e in range(2)
+    ]
+    row_of = (
+        lax.broadcasted_iota(jnp.int32, (shape[0], width), 0)
+        == jnp.where(node < 0, -1, node // shape[1])
+    ).astype(jnp.float32)
+    col_of = (lax.broadcasted_iota(jnp.int32, (shape[1], width), 0) == node % shape[1]).astype(jnp.float32)
+    at_node = dot(thick_ref[...].T, row_of, 1, 0)
+    gathers[0].start(0.9 * jnp.sum(at_node * col_of, axis=0, keepdims=True))
+    ocean = Ocean(
+        tools, state_ref, next_ref, halo_ref, weight_ref,
+        (row_src, row_land, col_src, col_land, row_send, row_recv, col_send, col_recv),
+    )
+    ocean.send_rows(0)
+    row_count, col_count = mean_ref.shape
+    item_row = (
+        lax.broadcasted_iota(jnp.int32, (row_count, items), 0)
+        == jnp.where(cell < 0, -1, cell // col_count)
+    ).astype(jnp.float32)
+    item_col = (lax.broadcasted_iota(jnp.int32, (col_count, items), 0) == cell % col_count).astype(jnp.float32)
+    item_slot = (lax.broadcasted_iota(jnp.int32, (width, items), 0) == slot_ref[...]).astype(jnp.float32)
+    cover = dot(item_row, item_col, 1, 1)
+    gathers[0].wait()
+    draft_item = dot(tall(slot_table(list_rows.at[0], me, peers, width)), item_slot, 1, 0)[0:1]
+    draft_field = dot(item_row * draft_item, item_col, 1, 1)
+    layers = [state_ref[i * levels] for i in range(4)]
+    layers += [mix_ref[...], wet_ref[...].astype(jnp.float32), cover, draft_field]
+    blocks, top_edges = top_exchange(tools, layers, top_src, top_land, top_send, top_recv)
+    top_next, melt_mean = top_steps(blocks, weight_ref, levels, next_ref)
+    mean_ref[...] = melt_mean
+    melt_item = jnp.sum(dot(melt_mean, item_col, 1, 0) * item_row, axis=0, keepdims=True)
+    gathers[1].start(dot(tall(melt_item), item_slot, 1, 1)[0:1])
+    for c in range(1, ocean.chunks):
+        ocean.send_rows(c)
     friction = fric_ref[...] * ground_ref[...].astype(jnp.float32) + 0.2
     cross = 0.9 * friction * coup_ref[...]
-    lane = lax.broadcasted_iota(jnp.int32, (1, width), 1)
-    row_of = (lax.broadcasted_iota(jnp.int32, (shape[0], width), 0) == jnp.where(node < 0, -1, node // shape[1])).astype(jnp.float32)
-    col_of = (lax.broadcasted_iota(jnp.int32, (shape[1], width), 0) == node % shape[1]).astype(jnp.float32)
-    gather.wait()
-    melt = jnp.zeros((1, width), jnp.float32)
-    for p in range(peers):
-        turn = lax.rem(CAP * (p - me) + width, width)
-        melt = jnp.where(lane // CAP == p, pltpu.roll(melt_rows[p], turn, 1), melt)
-    melt_node = lax.dot_general(
-        row_of * melt, col_of, (((1,), (1,)), ((), ())),
-        precision=lax.Precision.HIGHEST, preferred_element_type=jnp.float32,
-    )
+    ocean.send_columns(0)
+    gathers[1].wait()
+    melt = slot_table(list_rows.at[1], me, peers, width)
+    melt_node = dot(row_of * melt, col_of, 1, 1)
     thinned = thick_ref[...] * jnp.exp(-0.3 * melt_node)
     depth_visc = visc_ref[...] * thinned
     guess = [guess_ref[0], guess_ref[1]]
     rims = [Rim(tools, edge_src.at[e], edge_land.at[e], edge_send.at[e], edge_recv.at[e]) for e in range(3)]
     send_edges(rims[0], [depth_visc] + guess)
+    ocean.compute(0)
     values = rim_values(rims[0], 3, shape)
     weights = [0.5 * (depth_visc + beside) for beside in around(depth_visc, values[0])]
     diagonal = weights[0] + weights[1] + weights[2] + weights[3] + friction
@@ -341,12 +668,16 @@
     residual = [drive_ref[i] * thinned - image[i] for i in range(2)]
     precond = [residual[i] * scale for i in range(2)]
     send_edges(rims[1], precond)
+    if ocean.chunks > 1:
+        ocean.send_columns(1)
     edge_z = rim_values(rims[1], 2, shape)
     image = apply(precond, edge_z)
     scaled = [image[i] * scale for i in range(2)]
     part = half_sums(0, [(residual, precond), (precond, image)])
     send_edges(rims[2], scaled)
     edge_y = rim_values(rims[2], 2, shape)
+    if ocean.chunks > 1:
+        ocean.compute(1)
     norm, curve = whole_sums(0, part, 2)
     step = norm / curve
     velocity = [guess[i] + step * precond[i] for i in range(2)]
@@ -355,43 +686,75 @@
     edge = [tuple(z - step * y for z, y in zip(edge_z[i], edge_y[i])) for i in range(2)]
     next_image = apply(next_precond, edge)
     second = half_sums(1, [(residual, next_precond), (next_precond, next_image), (next_precond, image)])
+    for c in range(2, ocean.chunks):
+        ocean.send_columns(c)
     norm_next, own_curve, mixed = whole_sums(1, second, 3)
     ratio = norm_next / norm
     step = norm_next / (own_curve + 2.0 * ratio * mixed + ratio * ratio * curve)
     for i in range(2):
         vel_ref[i] = velocity[i] + step * (next_precond[i] + ratio * precond[i])
         res_ref[i] = residual[i] - step * (next_image[i] + ratio * image[i])
-    gather.finish()
+    for c in range(2, ocean.chunks):
+        ocean.compute(c)
+    for i in range(4):
+        next_ref[i * levels] = top_next[i]
+    ocean.finish()
+    for edge in top_edges:
+        edge.finish()
+    for gather in gathers:
+        gather.finish()
     part.finish()
     second.finish()
     for rim in rims:
         rim.finish()
 
 
-def ice_phase(melt_row, node_row, thickness, viscosity, friction, grounded, coupling, driving, first_guess):
+def whole_step(arrays, levels):
     n_grp, n_gx, n_gy = lax.axis_size("grp"), lax.axis_size("gx"), lax.axis_size("gy")
     peers = n_gx * n_gy
-    width = melt_row.shape[1]
-    cols = thickness.shape[1]
+    state, mix, guess = arrays[0], arrays[1], arrays[12]
+    width, cols = arrays[5].shape[1], guess.shape[2]
+    layer_total, row_count, col_count = state.shape
+    group = col_count // (2 * NSUB)
+    packs = layer_total // group
     vmem = pl.BlockSpec(memory_space=pltpu.VMEM)
     dma = pltpu.SemaphoreType.DMA
     f32 = jnp.float32
+
+    def buffer(*dims):
+        return pltpu.VMEM(dims, f32)
+
+    tile = (row_count, col_count)
     return pl.pallas_call(
-        ice_kernel,
-        out_shape=[jax.ShapeDtypeStruct(first_guess.shape, f32)] * 2,
-        in_specs=[vmem] * 9,
-        out_specs=[vmem] * 2,
+        functools.partial(step_kernel, levels),
+        out_shape=[jax.ShapeDtypeStruct(a.shape, f32) for a in (state, mix, guess, guess)],
+        in_specs=[vmem] * 13,
+        out_specs=[vmem] * 4,
         scratch_shapes=[
-            pltpu.VMEM((1, width), f32),
-            pltpu.VMEM((peers, 1, width), f32),
-            pltpu.VMEM((2, 8, cols), f32),
-            pltpu.VMEM((2, peers, 8, cols), f32),
-            pltpu.VMEM((2, 8, cols), f32),
-            pltpu.VMEM((2, n_grp - 1, 8, cols), f32),
-            pltpu.VMEM((3, 4, 8, cols), f32),
-            pltpu.VMEM((3, 4, 8, cols), f32),
-            dma((peers,)),
-            dma((peers,)),
+            buffer(layer_total, *tile),
+            buffer(3, 5, 2, *tile),
+            buffer(2, layer_total // 2, *tile),
+            buffer(2, layer_total // 2, *tile),
+            buffer(packs, 2, *tile),
+            buffer(2, packs, 2, *tile),
+            buffer(3, 4, *tile),
+            buffer(4, 4, *tile),
+            buffer(2, 1, width),
+            buffer(2, peers, 1, width),
+            buffer(2, 8, cols),
+            buffer(2, peers, 8, cols),
+            buffer(2, 8, cols),
+            buffer(2, n_grp - 1, 8, cols),
+            buffer(3, 4, 8, cols),
+            buffer(3, 4, 8, cols),
+            dma((3, 2)),
+            dma((3, 2)),
+            dma((3, 2)),
+            dma((3, 2)),
+            dma((2, 2)),
+            dma((2, 2)),
+            dma((2, peers)),
+            dma((2, peers)),
             dma((2, peers)),
             dma((2, peers)),
             dma((2, n_grp - 1)),
@@ -400,9 +763,9 @@
             dma((3, 4)),
         ],
         compiler_params=pltpu.CompilerParams(
-            collective_id=0, has_side_effects=True, vmem_limit_bytes=32 * 1024 * 1024
+            collective_id=0, has_side_effects=True, vmem_limit_bytes=40 * 1024 * 1024
         ),
-    )(melt_row, node_row, thickness, viscosity, friction, grounded, coupling, driving, first_guess)
+    )(*arrays)
 
 
 def shards(
@@ -421,69 +784,30 @@
     first_guess,
 ):
     field_count, level_count, row_count, col_count = ocean_state.shape
-    layers = field_count * level_count
-    owner = owner_node[0, 0]
-    valid = owner >= 0
-    safe_node = jnp.where(valid, owner, 0)
-    thick_flat = thickness.reshape(-1)
-    draft_send = jnp.where(valid, 0.9 * thick_flat[safe_node], 0.0)
-    draft_recv = lax.all_to_all(draft_send, ("gx", "gy"), split_axis=0, concat_axis=0, tiled=True)
-    columns = coast_column[0, 0]
-    slots = coast_slot[0, 0]
-    draft_item = draft_recv.reshape(-1)[slots]
-    cell_count = row_count * col_count
-    cover = jnp.zeros((cell_count,), jnp.float32).at[columns].set(1.0).reshape(row_count, col_count)
-    draft_field = (
-        jnp.zeros((cell_count,), jnp.float32)
-        .at[columns]
-        .set(draft_item)
-        .reshape(row_count, col_count)
+
+    def lane_row(values):
+        flat = values.reshape(1, -1)
+        return jnp.pad(flat, ((0, 0), (0, -flat.shape[1] % 128)), constant_values=-1)
+
+    fields, melt_mean, velocity, residual = whole_step(
+        (
+            ocean_state.reshape(-1, row_count, col_count),
+            diffusivity,
+            wet_mask,
+            lane_row(coast_column),
+            lane_row(coast_slot),
+            lane_row(owner_node),
+            thickness,
+            viscosity,
+            friction,
+            grounded,
+            coupling,
+            driving,
+            first_guess,
+        ),
+        level_count,
     )
-    wet_field = wet_mask.astype(jnp.float32)
-    total = jnp.zeros((row_count, col_count), jnp.float32)
-    fields = ocean_state
-    stacked = jnp.concatenate(
-        [
-            fields.reshape(layers, row_count, col_count),
-            diffusivity[None],
-            wet_field[None],
-            cover[None],
-            draft_field[None],
-        ],
-        0,
-    )
-    padded = padded_2(stacked, ((("grp", "gx"), 1), ("gy", 2)), NSUB)
-    current = padded[:layers].reshape(
-        field_count, level_count, row_count + 2 * NSUB, col_count + 2 * NSUB
-    )
-    for substep in range(NSUB):
-        stop_row = row_count + 2 * NSUB - substep
-        stop_col = col_count + 2 * NSUB - substep
-        diff_part = padded[layers, substep:stop_row, substep:stop_col]
-        wet_part = padded[layers + 1, substep:stop_row, substep:stop_col]
-        cover_part = padded[layers + 2, substep + 1 : stop_row - 1, substep + 1 : stop_col - 1]
-        draft_part = padded[layers + 3, substep + 1 : stop_row - 1, substep + 1 : stop_col - 1]
-        current, melt_rate = advance(current, diff_part, wet_part, cover_part, draft_part)
-        margin = NSUB - substep - 1
-        total = total + melt_rate[margin : margin + row_count, margin : margin + col_count]
-    fields = current
-    melt_mean = total / NSUB
-    lanes = 128 * (-(-owner.size // 128))
-    cells = jnp.arange(cell_count, dtype=jnp.int32)
-    melt_item = jnp.sum(
-        jnp.where(columns[:, None] == cells[None, :], melt_mean.reshape(1, -1), 0.0), axis=1
-    )
-    melt_row = jnp.sum(
-        jnp.where(
-            slots[:, None] == jnp.arange(lanes, dtype=jnp.int32)[None, :], melt_item[:, None], 0.0
-        ),
-        axis=0,
-    )[None]
-    node_row = jnp.pad(owner.reshape(1, -1), ((0, 0), (0, lanes - owner.size)), constant_values=-1)
-    velocity, residual = ice_phase(
-        melt_row, node_row, thickness, viscosity, friction, grounded, coupling, driving, first_guess
-    )
-    return (fields, melt_mean, velocity, residual)
+    return (fields.reshape(ocean_state.shape), melt_mean, velocity, residual)
 
 
 def solution(mesh):

time: 117 us -> 92.8 us (0.79)
  Pallas kernels: 28 us -> 79.5 us
  waiting for transfers between devices: 26.7 us -> 0 us
  other arithmetic: 22.1 us -> 0 us
  starting transfers between devices: 16.5 us -> 0 us
  local copies, waits for them, and re-layouts: 21.5 us -> 12.1 us
    pallas_call x1, Pallas kernels: 28 us -> 79.5 us  [whole_step(): pl.pallas_call(functools.partial(step_kernel, levels), out_shape=[jax.Sha...]
    ppermute x4 -> x0, waiting for transfers between devices: 20.4 us -> none  [the longest x2 10.5 us: padded_2(): lax.ppermute(lax.slice_in_dim(block, block.shape[dim] - width, None, axis...]
    add x4 -> x0, other arithmetic: 14 us -> none  [advance(): updated = fields + flux_sum]
    unnamed x42 -> x31, local copies, waits for them, and re-layouts: 3.5 us -> 12 us
    all_to_all x1 -> x0, starting transfers between devices: 8.31 us -> none  [shards(): lax.all_to_all(draft_send, ('gx', 'gy'), split_axis=0, concat_axis=0, til...]
    ppermute x4 -> x0, starting transfers between devices: 8.16 us -> none  [the longest x2 5.59 us: padded_2(): lax.ppermute(lax.slice_in_dim(block, block.shape[dim] - width, None, axis...]
    slice x5 -> x0, local copies, waits for them, and re-layouts: 7.29 us -> none  [the longest x3 5.19 us: padded_2(): lax.slice_in_dim(block, block.shape[dim] - width, None, axis=dim)]
    all_to_all x1 -> x0, waiting for transfers between devices: 6.3 us -> none  [shards(): lax.all_to_all(draft_send, ('gx', 'gy'), split_axis=0, concat_axis=0, til...]
  transfers between devices with their start and end apart: 5 -> 0, of which waited for: 4 -> 0; matrix products, arithmetic and copies ran while one was open for 4% -> 0% of each run, Pallas kernels for 0% -> 0%
where the time goes in v2:
time: 92.8 us; the launch traced here: 92.3 us
  Pallas kernels  79.5 us (86%)
  local copies, waits for them, and re-layouts  12.1 us (13%)
    pallas_call x1, Pallas kernels, whole_step(): pl.pallas_call(functools.partial(step_kernel, levels), out_shape=[jax.Sha...  79.5 us
    unnamed x31, local copies, waits for them, and re-layouts  12 us

profile of v2, /device:TPU:0, one launch (start us, length us, event | category | flops | bytes accessed | tf_op | source)
XLA Modules:
  0.0 92.3 jit_solution(2788507146172097156)
XLA Ops:
  0.6 0.0 copy-start.11
  0.6 0.0 copy-start.12
  0.7 0.6 copy-done.11
  1.3 0.0 copy-start.10
  1.3 0.0 copy-done.12
  1.3 0.7 copy-done.10
  2.0 0.1 copy.18
  2.1 0.0 copy-start.8
  2.1 0.0 copy-start.9
  2.1 0.1 reshape.26
  2.2 0.6 copy-done.8
  2.7 0.0 copy-done.9
  2.8 0.0 copy-start
  2.8 1.2 %copy-done = f32[4,60,8,128]{3,2,1,0:T(8,128)S(1)} copy-done((f32[4,60,8,128]{3,2,1,0:T(8,128)S(1)}, f32[4,60,8,128]{3,2,1,0:T(8,128)}, u32[]{:S(2)}) %copy-start) | copy-done | bytes 983064
  4.0 0.0 copy-start.1
  4.0 0.9 copy-done.1
  4.9 0.0 copy-start.2
  4.9 0.9 copy-done.2
  5.8 0.0 copy-start.3
  5.8 0.8 copy-done.3
  6.6 0.0 copy-start.4
  6.6 0.8 copy-done.4
  7.4 0.0 copy-start.5
  7.5 0.8 copy-done.5
  8.3 0.0 copy-start.6
  8.3 0.8 copy-done.6
  9.1 0.0 copy-start.7
  9.1 0.8 copy-done.7
  10.0 79.5 %shard_map.156 = (f32[240,8,128]{2,1,0:T(8,128)S(1)}, f32[8,128]{1,0:T(8,128)S(1)}, f32[2,128,128]{2,1,0:T(8,128)S(1)}, f32[2,128,128]{2,1,0:T(8,128)S(1)}) custom-call(f32[240,8,128]{2,1,0:T(8,128)S(1)} %bitcast.6, f32[8,128]{1,0:T(8,128)S(1)} %copy-done.8, s32[8,128]{1,0:T(8,128)S(1)} %copy-done.9, s32[1,128]{1,0:T(1,128)S(1)} %pad.11.cell_ref, ...), custom_call_target="tpu_custom_call" | custom-call | tf_op jit(solution)/shard_map/pallas_call | solution.py:728
  89.4 0.9 %copy.23 = f32[4,60,8,128]{3,2,1,0:T(8,128)} copy(f32[4,60,8,128]{3,2,1,0:T(8,128)S(1)} %bitcast.7) | data formatting | bytes 1966080
  90.4 0.6 copy.24
  91.0 0.7 copy.25
  91.6 0.7 copy.26
  (3 shorter events, 0.0 us)
Async XLA Ops:
  0.6 0.7 copy-start.11
  0.6 0.7 copy-start.12
  1.3 0.7 copy-start.10
  2.1 0.7 copy-start.8
  2.1 0.7 copy-start.9
  2.8 1.2 %copy-start = (f32[4,60,8,128]{3,2,1,0:T(8,128)S(1)}, f32[4,60,8,128]{3,2,1,0:T(8,128)}, u32[]{:S(2)}) copy-start(f32[4,60,8,128]{3,2,1,0:T(8,128)} %param.13) | copy-start | bytes 2949124
  4.0 0.9 copy-start.1
  4.9 0.9 copy-start.2
  5.8 0.8 copy-start.3
  6.6 0.8 copy-start.4
  7.4 0.8 copy-start.5
  8.3 0.8 copy-start.6
  9.1 0.8 copy-start.7

commit v3 on v2

--- a/solution.py
+++ b/solution.py
@@ -9,6 +9,7 @@
 
 NSUB = 4
 CAP = 4
+BATCH = 8
 MESH = pl.DeviceIdType.MESH
 
 
@@ -329,6 +330,20 @@
         for weight, side in zip(weights[0], sides):
             total = total + weight[t] * side[t]
         out.append(total)
+    return out
+
+
+def spread_rim(pair, weights, rim, tiles):
+    width = pair[0].shape[1]
+    lane = lax.broadcasted_iota(jnp.int32, pair[0].shape, 1)
+    up, down = row_ring(pair)
+    out = []
+    for t in range(tiles):
+        right = pltpu.roll(jnp.where(lane == 0, rim[t], pair[t]), width - 1, 1)
+        left = pltpu.roll(jnp.where(lane == width - 1, rim[t], pair[t]), 1, 1)
+        rows = weights[0][0][t] * up[t] + weights[0][1][t] * down[t]
+        cols = weights[0][2][t] * right + weights[0][3][t] * left
+        out.append(weights[1][t] * pair[t] + (rows + cols))
     return out
 
 
@@ -445,14 +460,25 @@
                     stages.append(spread(stages[-1], weights))
                 wings.append(stages)
             weights = weights_of(1)
-            for j in range(self.group):
-                place = 2 * NSUB * j
-                pair = [self.state[v * self.group + j], self.halo[v * self.group + j]]
+            ends = [
+                [joined(wings[0][s][t], wings[1][s][t]) for t in range(2)] for s in range(NSUB)
+            ]
+            width = ends[0][0].shape[1]
+            for first in range(0, self.group, BATCH):
+                batch = range(first, min(first + BATCH, self.group))
+                pairs = [
+                    [self.state[v * self.group + j], self.halo[v * self.group + j]] for j in batch
+                ]
                 for s in range(NSUB):
-                    west = column(wings[0][s], place + NSUB - 1)
-                    east = column(wings[1][s], place + NSUB)
-                    pair = spread(pair, weights, west, east, 1 if s == NSUB - 1 else 2)
-                self.next[v * self.group + j] = pair[0]
+                    tiles = 1 if s == NSUB - 1 else 2
+                    moved = []
+                    for j, pair in zip(batch, pairs):
+                        turn = (2 * width - NSUB - 2 * NSUB * j) % width
+                        rim = [pltpu.roll(ends[s][t], turn, 1) for t in range(tiles)]
+                        moved.append(spread_rim(pair, weights, rim, tiles))
+                    pairs = moved
+                for j, pair in zip(batch, pairs):
+                    self.next[v * self.group + j] = pair[0]
 
         self.loop(c, step)
 
@@ -521,12 +547,24 @@
 
 def step_kernel(
     levels,
-    state_ref,
+    state_hbm,
     mix_ref,
     wet_ref,
     cell_ref,
     slot_ref,
     node_ref,
+    thick_hbm,
+    visc_hbm,
+    fric_hbm,
+    ground_hbm,
+    coup_hbm,
+    drive_hbm,
+    guess_hbm,
+    next_ref,
+    mean_ref,
+    vel_ref,
+    res_ref,
+    state_ref,
     thick_ref,
     visc_ref,
     fric_ref,
@@ -534,10 +572,7 @@
     coup_ref,
     drive_ref,
     guess_ref,
-    next_ref,
-    mean_ref,
-    vel_ref,
-    res_ref,
+    load_sems,
     halo_ref,
     weight_ref,
     row_src,
@@ -571,6 +606,19 @@
 ):
     tools = device_tools(("grp", "gx", "gy"))
     grp, gx, gy, n_grp, n_gx, n_gy, sides = tools
+    pairs = (
+        (thick_hbm, thick_ref),
+        (state_hbm, state_ref),
+        (visc_hbm, visc_ref),
+        (guess_hbm, guess_ref),
+        (drive_hbm, drive_ref),
+        (fric_hbm, fric_ref),
+        (ground_hbm, ground_ref),
+        (coup_hbm, coup_ref),
+    )
+    loads = [pltpu.make_async_copy(a, b, load_sems.at[i]) for i, (a, b) in enumerate(pairs)]
+    for load in loads:
+        load.start()
     enter(tools)
     me = gx * n_gy + gy
     peers = n_gx * n_gy
@@ -587,12 +635,14 @@
         == jnp.where(node < 0, -1, node // shape[1])
     ).astype(jnp.float32)
     col_of = (lax.broadcasted_iota(jnp.int32, (shape[1], width), 0) == node % shape[1]).astype(jnp.float32)
+    loads[0].wait()
     at_node = dot(thick_ref[...].T, row_of, 1, 0)
     gathers[0].start(0.9 * jnp.sum(at_node * col_of, axis=0, keepdims=True))
     ocean = Ocean(
         tools, state_ref, next_ref, halo_ref, weight_ref,
         (row_src, row_land, col_src, col_land, row_send, row_recv, col_send, col_recv),
     )
+    loads[1].wait()
     ocean.send_rows(0)
     row_count, col_count = mean_ref.shape
     item_row = (
@@ -614,6 +664,8 @@
     gathers[1].start(dot(tall(melt_item), item_slot, 1, 1)[0:1])
     for c in range(1, ocean.chunks):
         ocean.send_rows(c)
+    for load in loads[2:]:
+        load.wait()
     friction = fric_ref[...] * ground_ref[...].astype(jnp.float32) + 0.2
     cross = 0.9 * friction * coup_ref[...]
     ocean.send_columns(0)
@@ -718,6 +770,7 @@
     group = col_count // (2 * NSUB)
     packs = layer_total // group
     vmem = pl.BlockSpec(memory_space=pltpu.VMEM)
+    hbm = pl.BlockSpec(memory_space=pltpu.HBM)
     dma = pltpu.SemaphoreType.DMA
     f32 = jnp.float32
 
@@ -728,9 +781,11 @@
     return pl.pallas_call(
         functools.partial(step_kernel, levels),
         out_shape=[jax.ShapeDtypeStruct(a.shape, f32) for a in (state, mix, guess, guess)],
-        in_specs=[vmem] * 13,
+        in_specs=[hbm, vmem, vmem, vmem, vmem, vmem] + [hbm] * 7,
         out_specs=[vmem] * 4,
         scratch_shapes=[
+            *(pltpu.VMEM(arrays[i].shape, arrays[i].dtype) for i in (0, 6, 7, 8, 9, 10, 11, 12)),
+            dma((8,)),
             buffer(layer_total, *tile),
             buffer(3, 5, 2, *tile),
             buffer(2, layer_total // 2, *tile),
@@ -763,7 +818,7 @@
             dma((3, 4)),
         ],
         compiler_params=pltpu.CompilerParams(
-            collective_id=0, has_side_effects=True, vmem_limit_bytes=40 * 1024 * 1024
+            collective_id=0, has_side_effects=True, vmem_limit_bytes=56 * 1024 * 1024
         ),
     )(*arrays)
 

time: 92.8 us -> 66.1 us (0.71)
  Pallas kernels: 79.5 us -> 58.4 us
  local copies, waits for them, and re-layouts: 12.1 us -> 6.82 us
    pallas_call x1, Pallas kernels: 79.5 us -> 58.4 us  [whole_step(): pl.pallas_call(functools.partial(step_kernel, levels), out_shape=[jax.Sha...]
    unnamed x31 -> x17, local copies, waits for them, and re-layouts: 12 us -> 5.18 us
    pad x3, local copies, waits for them, and re-layouts: 0.02 us -> 1.55 us  [lane_row(): jnp.pad(flat, ((0, 0), (0, -flat.shape[1] % 128)), constant_values=-1)]
where the time goes in v3:
time: 66.1 us; the launch traced here: 65.9 us
  Pallas kernels  58.4 us (88%)
  local copies, waits for them, and re-layouts  6.82 us (10%)
  between operations  0.68 us (1%)
    pallas_call x1, Pallas kernels, whole_step(): pl.pallas_call(functools.partial(step_kernel, levels), out_shape=[jax.Sha...  58.4 us
    unnamed x17, local copies, waits for them, and re-layouts  5.18 us
    pad x3, local copies, waits for them, and re-layouts, lane_row(): jnp.pad(flat, ((0, 0), (0, -flat.shape[1] % 128)), constant_values=-1)  1.55 us

profile of v3, /device:TPU:0, one launch (start us, length us, event | category | flops | bytes accessed | tf_op | source)
XLA Modules:
  0.0 65.9 jit_solution(1908167662044373065)
XLA Ops:
  0.6 0.0 copy-start.4
  0.6 0.0 copy-start.5
  0.7 0.6 copy-done.4
  1.3 0.0 copy-start.3
  1.3 0.5 pad.11.cell_ref
  1.8 0.0 copy-done.5
  1.8 0.5 pad.12.slot_ref
  2.3 0.0 copy-done.3
  2.3 0.1 copy.18
  2.4 0.1 reshape.26
  2.5 0.5 pad.13.node_ref
  3.0 58.4 %shard_map.156 = (f32[240,8,128]{2,1,0:T(8,128)}, f32[8,128]{1,0:T(8,128)}, f32[2,128,128]{2,1,0:T(8,128)}, f32[2,128,128]{2,1,0:T(8,128)}) custom-call(f32[240,8,128]{2,1,0:T(8,128)} %bitcast.6, f32[8,128]{1,0:T(8,128)} %mix_ref.1, s32[8,128]{1,0:T(8,128)} %wet_ref.1, s32[1,128]{1,0:T(1,128)} %pad.11.cell_ref, s32[1,128]{1,0:T(1,128)} %pad.12.slot_ref, ...), custom_call_target="tpu_custom_call" | custom-call | tf_op jit(solution)/shard_map/pallas_call | solution.py:781
  61.4 0.0 copy-start.2
  61.4 0.0 copy-start.1
  61.4 2.2 %copy.23 = f32[4,60,8,128]{3,2,1,0:T(8,128)} copy(f32[4,60,8,128]{3,2,1,0:T(8,128)} %bitcast.7) | data formatting | bytes 1966080
  63.7 0.0 copy-done.2
  63.7 0.6 copy.24
  64.3 0.0 copy-done.1
  64.3 0.0 copy-start
  64.3 0.7 copy.25
  64.9 0.3 copy-done
  65.2 0.7 copy.26
Async XLA Ops:
  0.6 0.7 copy-start.4
  0.6 1.2 %copy-start.5 = (s32[1,1,32]{2,1,0:T(1,128)S(1)}, s32[1,1,32]{2,1,0:T(1,128)}, u32[]{:S(2)}) copy-start(s32[1,1,32]{2,1,0:T(1,128)} %param.17) | copy-start | bytes 388
  1.3 1.0 %copy-start.3 = (s32[1,1,16,4]{2,3,1,0:T(4,128)S(1)}, s32[1,1,16,4]{2,3,1,0:T(4,128)}, u32[]{:S(2)}) copy-start(s32[1,1,16,4]{2,3,1,0:T(4,128)} %param.18) | copy-start | bytes 772
  61.4 2.3 %copy-start.2 = (f32[8,128]{1,0:T(8,128)S(1)}, f32[8,128]{1,0:T(8,128)}, u32[]{:S(2)}) copy-start(f32[8,128]{1,0:T(8,128)} %get-tuple-element.17) | copy-start | bytes 12292
  61.4 2.9 %copy-start.1 = (f32[2,128,128]{2,1,0:T(8,128)S(1)}, f32[2,128,128]{2,1,0:T(8,128)}, u32[]{:S(2)}) copy-start(f32[2,128,128]{2,1,0:T(8,128)} %get-tuple-element.18) | copy-start | bytes 393220
  64.3 1.0 %copy-start = (f32[2,128,128]{2,1,0:T(8,128)S(1)}, f32[2,128,128]{2,1,0:T(8,128)}, u32[]{:S(2)}) copy-start(f32[2,128,128]{2,1,0:T(8,128)} %get-tuple-element.19) | copy-start | bytes 393220

commit v4 on v3

--- a/solution.py
+++ b/solution.py
@@ -727,6 +727,8 @@
     scaled = [image[i] * scale for i in range(2)]
     part = half_sums(0, [(residual, precond), (precond, image)])
     send_edges(rims[2], scaled)
+    for c in range(2, ocean.chunks):
+        ocean.send_columns(c)
     edge_y = rim_values(rims[2], 2, shape)
     if ocean.chunks > 1:
         ocean.compute(1)
@@ -739,15 +741,13 @@
     next_image = apply(next_precond, edge)
     second = half_sums(1, [(residual, next_precond), (next_precond, next_image), (next_precond, image)])
     for c in range(2, ocean.chunks):
-        ocean.send_columns(c)
+        ocean.compute(c)
     norm_next, own_curve, mixed = whole_sums(1, second, 3)
     ratio = norm_next / norm
     step = norm_next / (own_curve + 2.0 * ratio * mixed + ratio * ratio * curve)
     for i in range(2):
         vel_ref[i] = velocity[i] + step * (next_precond[i] + ratio * precond[i])
         res_ref[i] = residual[i] - step * (next_image[i] + ratio * image[i])
-    for c in range(2, ocean.chunks):
-        ocean.compute(c)
     for i in range(4):
         next_ref[i * levels] = top_next[i]
     ocean.finish()

time: 66.1 us -> 62.4 us (0.944)
  Pallas kernels: 58.4 us -> 54.7 us
    pallas_call x1, Pallas kernels: 58.4 us -> 54.7 us  [whole_step(): pl.pallas_call(functools.partial(step_kernel, levels), out_shape=[jax.Sha...]
where the time goes in v4:
time: 62.4 us; the launch traced here: 62.2 us
  Pallas kernels  54.7 us (88%)
  local copies, waits for them, and re-layouts  6.82 us (11%)
  between operations  0.68 us (1%)
    pallas_call x1, Pallas kernels, whole_step(): pl.pallas_call(functools.partial(step_kernel, levels), out_shape=[jax.Sha...  54.7 us
    unnamed x17, local copies, waits for them, and re-layouts  5.18 us
    pad x3, local copies, waits for them, and re-layouts, lane_row(): jnp.pad(flat, ((0, 0), (0, -flat.shape[1] % 128)), constant_values=-1)  1.55 us

profile of v4, /device:TPU:0, one launch (start us, length us, event | category | flops | bytes accessed | tf_op | source)
XLA Modules:
  0.0 62.2 jit_solution(3257324397844199888)
XLA Ops:
  0.6 0.0 copy-start.4
  0.6 0.0 copy-start.5
  0.7 0.6 %copy-done.4 = s32[1,1,32]{2,1,0:T(1,128)S(1)} copy-done((s32[1,1,32]{2,1,0:T(1,128)S(1)}, s32[1,1,32]{2,1,0:T(1,128)}, u32[]{:S(2)}) %copy-start.4) | copy-done | bytes 152
  1.3 0.0 copy-start.3
  1.3 0.5 pad.11.cell_ref
  1.8 0.0 copy-done.5
  1.8 0.5 pad.12.slot_ref
  2.3 0.0 copy-done.3
  2.3 0.1 copy.18
  2.4 0.1 reshape.26
  2.5 0.5 pad.13.node_ref
  3.0 54.7 %shard_map.156 = (f32[240,8,128]{2,1,0:T(8,128)}, f32[8,128]{1,0:T(8,128)}, f32[2,128,128]{2,1,0:T(8,128)}, f32[2,128,128]{2,1,0:T(8,128)}) custom-call(f32[240,8,128]{2,1,0:T(8,128)} %bitcast.6, f32[8,128]{1,0:T(8,128)} %mix_ref.1, s32[8,128]{1,0:T(8,128)} %wet_ref.1, s32[1,128]{1,0:T(1,128)} %pad.11.cell_ref, s32[1,128]{1,0:T(1,128)} %pad.12.slot_ref, ...), custom_call_target="tpu_custom_call" | custom-call | tf_op jit(solution)/shard_map/pallas_call | solution.py:781
  57.7 0.0 copy-start.2
  57.7 0.0 copy-start.1
  57.7 2.2 %copy.23 = f32[4,60,8,128]{3,2,1,0:T(8,128)} copy(f32[4,60,8,128]{3,2,1,0:T(8,128)} %bitcast.7) | data formatting | bytes 1966080
  60.0 0.0 copy-done.2
  60.0 0.6 copy.24
  60.6 0.0 copy-done.1
  60.6 0.0 copy-start
  60.6 0.7 %copy.25 = f32[2,128,128]{2,1,0:T(8,128)} copy(f32[2,128,128]{2,1,0:T(8,128)S(1)} %copy-done.1) | data formatting | bytes 262144
  61.2 0.3 copy-done
  61.5 0.7 %copy.26 = f32[2,128,128]{2,1,0:T(8,128)} copy(f32[2,128,128]{2,1,0:T(8,128)S(1)} %copy-done) | data formatting | bytes 262144
Async XLA Ops:
  0.6 0.7 %copy-start.4 = (s32[1,1,32]{2,1,0:T(1,128)S(1)}, s32[1,1,32]{2,1,0:T(1,128)}, u32[]{:S(2)}) copy-start(s32[1,1,32]{2,1,0:T(1,128)} %param.16) | copy-start | bytes 388
  0.6 1.2 %copy-start.5 = (s32[1,1,32]{2,1,0:T(1,128)S(1)}, s32[1,1,32]{2,1,0:T(1,128)}, u32[]{:S(2)}) copy-start(s32[1,1,32]{2,1,0:T(1,128)} %param.17) | copy-start | bytes 388
  1.3 1.0 %copy-start.3 = (s32[1,1,16,4]{2,3,1,0:T(4,128)S(1)}, s32[1,1,16,4]{2,3,1,0:T(4,128)}, u32[]{:S(2)}) copy-start(s32[1,1,16,4]{2,3,1,0:T(4,128)} %param.18) | copy-start | bytes 772
  57.7 2.3 %copy-start.2 = (f32[8,128]{1,0:T(8,128)S(1)}, f32[8,128]{1,0:T(8,128)}, u32[]{:S(2)}) copy-start(f32[8,128]{1,0:T(8,128)} %get-tuple-element.17) | copy-start | bytes 12292
  57.7 2.9 %copy-start.1 = (f32[2,128,128]{2,1,0:T(8,128)S(1)}, f32[2,128,128]{2,1,0:T(8,128)}, u32[]{:S(2)}) copy-start(f32[2,128,128]{2,1,0:T(8,128)} %get-tuple-element.18) | copy-start | bytes 393220
  60.6 1.0 %copy-start = (f32[2,128,128]{2,1,0:T(8,128)S(1)}, f32[2,128,128]{2,1,0:T(8,128)}, u32[]{:S(2)}) copy-start(f32[2,128,128]{2,1,0:T(8,128)} %get-tuple-element.19) | copy-start | bytes 393220
